TPU v7x, 512 devices: a whole 4x4x16 slice. The times are simulated.
512 devices in a mesh: dp: 64 (over y, z), mp: 8 (over x, core).
Axes of the slice: x: 4, y: 4, z: 16, core: 2. Of those that a mesh axis runs over, the one named last changes fastest.
Arguments:
- tokens: bfloat16 [32768, 8192], P('dp', 'mp'), may hold values from -6 to 6
- base_weight: bfloat16 [8192, 1024], P('mp'), may hold values from -0.0625 to 0.0625
- adapter_a: bfloat16 [128, 8192, 64], P('dp', 'mp'), may hold values from -0.0625 to 0.0625
- adapter_b: bfloat16 [128, 64, 1024], P('dp', None, 'mp'), may hold values from -0.75 to 0.75
- row_ids: int32 [32768], P('dp'), may hold values from 0 to 127, as said below
- panel_of: int32 [128], replicated, may hold values from 0 to 127, as said below
- stop_flags: int32 [128], P('dp'), may hold values 0 or 1
- upstream: bfloat16 [32768, 1024], P('dp', 'mp'), may hold values from -6 to 6
Outputs:
- projected: bfloat16 [32768, 1024], P('dp', 'mp')
- token_input_gradient: bfloat16 [32768, 8192], P('dp', 'mp')
- down_gradient: bfloat16 [128, 8192, 64], P('dp', 'mp')
- up_gradient: bfloat16 [128, 64, 1024], P('dp', None, 'mp')
Inputs may be any that keep to these rules, and one draw needn't show every extreme that they name: `row_ids`: within the rows of one index of dp the ids never fall; those rows name exactly 64 adapters, one of the panels of every owner (owner = panel_of[id] // 2); at most 10 rows of one index of dp belong to the panels of one owner, and every index of dp has some owner with exactly 10 of its rows. `panel_of`: each panel number appears once; panel p is owned by index p // 2 of dp.
All inputs are finite; a program needn't handle non-finite values. No bound on the sum of `stop_flags` on one device may be relied on, other than what follows from the above.
Results may differ from a plain program's by a relative error of at most 0.0055.
Values may be sent and summed in bfloat16 or wider, within the bound.
A program may use at most 64 MiB of HBM per device.

v0:
```python
import jax
import jax.numpy as jnp
from jax import lax
from jax.sharding import PartitionSpec as P

adapter_scale = 2.0


def shards(tokens, base_weight, adapter_a, adapter_b, row_ids, panel_of, stop_flags, upstream):
    local_rows = tokens.shape[0]
    feature_shard = tokens.shape[1]
    value_shard = upstream.shape[1]
    panel_holders = lax.axis_size("dp")
    per_owner = adapter_a.shape[0]
    slot_capacity = 5 * local_rows // (4 * panel_holders)
    slot_table = panel_holders * slot_capacity
    columns = base_weight
    frozen_output = lax.psum_scatter(
        lax.dot_general(
            columns, tokens, (((0,), (1,)), ((), ())), preferred_element_type=jnp.float32
        ),
        "mp",
        scatter_dimension=0,
        tiled=True,
    ).T
    columns = base_weight
    frozen_gradient = lax.dot_general(
        lax.all_gather(upstream, "mp", axis=1, tiled=True),
        columns,
        (((1,), (1,)), ((), ())),
        preferred_element_type=jnp.float32,
    )
    all_panels = panel_of.shape[0]
    matches = row_ids[:, None] == jnp.arange(all_panels, dtype=jnp.int32)[None, :]
    panel = jnp.sum(jnp.where(matches, panel_of[None, :], 0), axis=1)
    owner = panel // per_owner
    within = panel % per_owner
    hits = (owner[:, None] == jnp.arange(panel_holders, dtype=jnp.int32)[None, :]).astype(jnp.int32)
    earlier = jnp.cumsum(hits, axis=0) - hits
    position = jnp.sum(earlier * hits, axis=1)
    target_rows = owner * slot_capacity + position
    source = (
        jnp.zeros((slot_table,), jnp.int32)
        .at[target_rows]
        .set(jnp.arange(local_rows, dtype=jnp.int32))
    )
    filled = jnp.zeros((slot_table,), jnp.bool_).at[target_rows].set(True)
    send_tokens = jnp.where(filled[:, None], tokens[source], 0).reshape(
        panel_holders, slot_capacity, feature_shard
    )
    send_upstream = jnp.where(filled[:, None], upstream[source], 0).reshape(
        panel_holders, slot_capacity, value_shard
    )
    send_panel = jnp.where(filled, within[source], -1).reshape(panel_holders, slot_capacity)
    got_tokens, got_upstream, got_panel = (
        lax.all_to_all(send_tokens, "dp", split_axis=0, concat_axis=0, tiled=True),
        lax.all_to_all(send_upstream, "dp", split_axis=0, concat_axis=0, tiled=True),
        lax.all_to_all(send_panel, "dp", split_axis=0, concat_axis=0, tiled=True),
    )
    incoming_rows = got_tokens.reshape(slot_table, feature_shard)
    incoming_gradients = got_upstream.reshape(slot_table, value_shard)
    selected_adapter = (
        got_panel.reshape(slot_table)[:, None] == jnp.arange(per_owner, dtype=jnp.int32)[None, :]
    )
    inner_part = jnp.sum(
        jnp.where(
            selected_adapter[:, :, None],
            jnp.einsum("cd,pdr->cpr", incoming_rows, adapter_a, preferred_element_type=jnp.float32),
            0.0,
        ),
        axis=1,
    )
    back_part = jnp.sum(
        jnp.where(
            selected_adapter[:, :, None],
            jnp.einsum(
                "ck,prk->cpr", incoming_gradients, adapter_b, preferred_element_type=jnp.float32
            ),
            0.0,
        ),
        axis=1,
    )
    active_mask = (1 - stop_flags).astype(jnp.float32)
    rank_activation, backward_result = lax.psum((inner_part, back_part), "mp")
    spread_inner = jnp.where(
        selected_adapter[:, :, None], rank_activation.astype(jnp.bfloat16)[:, None, :], 0
    )
    adapter_delta = (
        adapter_scale
        * jnp.einsum("cpr,prk->ck", spread_inner, adapter_b, preferred_element_type=jnp.float32)
    ).astype(jnp.bfloat16)
    panel_up_gradient = (
        adapter_scale
        * active_mask[:, None, None]
        * jnp.einsum(
            "cpr,ck->prk", spread_inner, incoming_gradients, preferred_element_type=jnp.float32
        )
    ).astype(jnp.bfloat16)
    adapter_delta, up_gradient = (
        adapter_delta.reshape(panel_holders, slot_capacity, value_shard),
        panel_up_gradient,
    )
    spread_back = jnp.where(
        selected_adapter[:, :, None], backward_result.astype(jnp.bfloat16)[:, None, :], 0
    )
    adapter_gradient = (
        adapter_scale
        * jnp.einsum("cpr,pdr->cd", spread_back, adapter_a, preferred_element_type=jnp.float32)
    ).astype(jnp.bfloat16)
    panel_down_gradient = (
        adapter_scale
        * active_mask[:, None, None]
        * jnp.einsum("cd,cpr->pdr", incoming_rows, spread_back, preferred_element_type=jnp.float32)
    ).astype(jnp.bfloat16)
    adapter_gradient, down_gradient = (
        adapter_gradient.reshape(panel_holders, slot_capacity, feature_shard),
        panel_down_gradient,
    )
    adapter_backward, returned_gradient = (
        lax.all_to_all(adapter_delta, "dp", split_axis=0, concat_axis=0, tiled=True),
        lax.all_to_all(adapter_gradient, "dp", split_axis=0, concat_axis=0, tiled=True),
    )
    adapter_rows = adapter_backward.reshape(slot_table, value_shard)[target_rows]
    grad_rows = returned_gradient.reshape(slot_table, feature_shard)[target_rows]
    projected = (frozen_output + adapter_rows.astype(jnp.float32)).astype(jnp.bfloat16)
    token_input_gradient = (frozen_gradient + grad_rows.astype(jnp.float32)).astype(jnp.bfloat16)
    return (projected, token_input_gradient, down_gradient, up_gradient)


def solution(mesh):
    placed = (
        P("dp", "mp"),
        P("mp", None),
        P("dp", "mp", None),
        P("dp", None, "mp"),
        P("dp"),
        P(),
        P("dp"),
        P("dp", "mp"),
    )
    return jax.shard_map(
        shards,
        mesh=mesh,
        in_specs=placed,
        out_specs=(P("dp", "mp"), P("dp", "mp"), P("dp", "mp", None), P("dp", None, "mp")),
        check_vma=False,
    )
```

profile of v0, /device:TPU:6, one launch (start us, length us, event | category | flops | bytes accessed | tf_op | source)
XLA Modules:
  0.0 364.1 jit_solution(9920519992507687234)
XLA Ops:
  7.2 1.1 select_reduce_fusion.1
  8.3 1.2 reduce-window.6
  9.5 0.2 slice_reduce_fusion
  9.8 0.1 fusion.18
  10.0 2.4 scatter_custom_fusion.1
  12.4 4.3 %gather_fusion = s32[640]{0:T(1024)S(1)} fusion(s32[512]{0:T(512)S(1)} %get-tuple-element.22, s32[1024]{0:T(1024)S(1)} %pad_clamp_fusion.1), kind=kCustom, calls=%fused_computation | custom fusion | bytes 7680 | tf_op jit(solution)/shard_map/gather | solution.py:54
  16.8 2.4 scatter_custom_fusion
  19.3 0.7 all_to_all.18
  20.0 18.7 %all-to-all-start = ((s32[64,1,10]{2,1,0:T(1,128)}), s32[64,1,10]{2,1,0:T(1,128)S(1)}, u32[]{:S(2)}, u32[]{:S(2)}) async-start(s32[64,1,10]{2,1,0:T(1,128)} %bitcast.6), calls=%async_computation.1 | async-start | bytes 65536 | tf_op jit(solution)/shard_map/all_to_all | solution.py:58
  38.7 0.1 broadcast_in_dim.123
  38.9 2.5 gather_fusion.3
  41.4 1.0 gather.24
  42.4 0.9 broadcast_select_fusion.1
  43.3 9.8 %all-to-all-done = s32[64,1,10]{2,1,0:T(1,128)S(1)} async-done(((s32[64,1,10]{2,1,0:T(1,128)}), s32[64,1,10]{2,1,0:T(1,128)S(1)}, u32[]{:S(2)}, u32[]{:S(2)}) %all-to-all-start) | async-done | bytes 2592 | tf_op jit(solution)/shard_map/all_to_all | solution.py:58
  53.1 5.4 %all-to-all-start.3 = ((bf16[64,10,128]{2,1,0:T(8,128)(2,1)}), bf16[64,10,128]{2,1,0:T(8,128)(2,1)S(1)}, u32[]{:S(2)}, u32[]{:S(2)}) async-start(bf16[64,10,128]{2,1,0:T(8,128)(2,1)} %broadcast_select_fusion.1), calls=%async_computation.4 | async-start | bytes 524288 | tf_op jit(solution)/shard_map/all_to_all | solution.py:57
  58.5 3.5 gather_fusion.1
  61.9 3.6 gather.21
  65.5 3.1 broadcast_select_fusion
  68.7 10.2 %all-to-all-done.3 = bf16[64,10,128]{2,1,0:T(8,128)(2,1)S(1)} async-done(((bf16[64,10,128]{2,1,0:T(8,128)(2,1)}), bf16[64,10,128]{2,1,0:T(8,128)(2,1)S(1)}, u32[]{:S(2)}, u32[]{:S(2)}) %all-to-all-start.3) | async-done | bytes 163872 | tf_op jit(solution)/shard_map/all_to_all | solution.py:57
  78.9 6.7 %all-to-all-start.1 = ((bf16[64,10,1024]{2,1,0:T(8,128)(2,1)}), bf16[64,10,1024]{2,1,0:T(8,128)(2,1)}, u32[]{:S(2)}, u32[]{:S(2)}) async-start(bf16[64,10,1024]{2,1,0:T(8,128)(2,1)} %broadcast_select_fusion), calls=%async_computation.2 | async-start | bytes 4194304 | tf_op jit(solution)/shard_map/all_to_all | solution.py:56
  85.7 2.7 fusion.40
  88.4 0.5 broadcast.224
  88.9 0.7 reduce.5
  89.6 0.1 eq.64
  89.9 0.9 fusion.5
  90.7 91.8 %all-to-all-done.1 = bf16[64,10,1024]{2,1,0:T(8,128)(2,1)} async-done(((bf16[64,10,1024]{2,1,0:T(8,128)(2,1)}), bf16[64,10,1024]{2,1,0:T(8,128)(2,1)}, u32[]{:S(2)}, u32[]{:S(2)}) %all-to-all-start.1) | async-done | bytes 1310752 | tf_op jit(solution)/shard_map/all_to_all | solution.py:56
  182.6 2.6 reshape.163
  185.1 1.5 fusion.41
  186.7 24.5 %all-reduce.2 = (bf16[640,64]{0,1:T(8,128)(2,1)S(1)}, bf16[640,64]{0,1:T(8,128)(2,1)S(1)}) all-reduce(f32[640,64]{0,1:T(8,128)S(1)} %select_reduce_fusion, f32[640,64]{0,1:T(8,128)} %fusion.5), channel_id=1, replica_groups=mesh['dp'=64,'mp'=8] {'mp'}, use_global_device_ids=true, to_apply=%region_8.9 | all-reduce | flops 81920 | bytes 491520 | tf_op jit(solution)/shard_map/psum | solution.py:84
  211.2 0.2 fusion.4
  211.5 0.8 reshape.164
  212.2 9.6 %all-to-all-start.2 = ((bf16[64,10,128]{2,1,0:T(8,128)(2,1)}), bf16[64,10,128]{2,1,0:T(8,128)(2,1)}, u32[]{:S(2)}, u32[]{:S(2)}) async-start(bf16[64,10,128]{2,1,0:T(8,128)(2,1)} %reshape.164), calls=%async_computation.3 | async-start | bytes 524288 | tf_op jit(solution)/shard_map/all_to_all | solution.py:120
  221.8 1.5 fusion
  223.3 1.6 reshape.167
  224.9 18.6 %all-to-all-done.2 = bf16[64,10,128]{2,1,0:T(8,128)(2,1)} async-done(((bf16[64,10,128]{2,1,0:T(8,128)(2,1)}), bf16[64,10,128]{2,1,0:T(8,128)(2,1)}, u32[]{:S(2)}, u32[]{:S(2)}) %all-to-all-start.2) | async-done | bytes 163872 | tf_op jit(solution)/shard_map/all_to_all | solution.py:120
  243.4 6.8 %all-to-all-start.4 = ((bf16[64,10,1024]{2,1,0:T(8,128)(2,1)}), bf16[64,10,1024]{2,1,0:T(8,128)(2,1)}, u32[]{:S(2)}, u32[]{:S(2)}) async-start(bf16[64,10,1024]{2,1,0:T(8,128)(2,1)} %reshape.167), calls=%async_computation.5 | async-start | bytes 4194304 | tf_op jit(solution)/shard_map/all_to_all | solution.py:121
  250.3 0.7 all-gather.2.cloned.1.call-update
  251.1 2.6 reshape.233
  253.6 1.8 fusion.6
  255.4 1.1 fusion.3
  256.5 1.0 reshape.165
  257.5 1.3 gather_fusion.2
  259.0 1.0 fusion.7
  260.0 0.8 copy.24
  260.7 87.4 %all-to-all-done.4 = bf16[64,10,1024]{2,1,0:T(8,128)(2,1)} async-done(((bf16[64,10,1024]{2,1,0:T(8,128)(2,1)}), bf16[64,10,1024]{2,1,0:T(8,128)(2,1)}, u32[]{:S(2)}, u32[]{:S(2)}) %all-to-all-start.4) | async-done | bytes 1310752 | tf_op jit(solution)/shard_map/all_to_all | solution.py:121
  348.1 2.6 reshape.168
  350.7 2.8 gather_fusion.4
  353.4 3.8 %add_convert_fusion = bf16[512,1024]{1,0:T(8,128)(2,1)} fusion(bf16[512,1024]{1,0:T(8,128)(2,1)} %gather_fusion.4, bf16[512,1024]{1,0:T(8,128)(2,1)} %all-gather.2.cloned.1.call-done, bf16[1024,1024]{1,0:T(8,128)(2,1)S(1)} %copy-done), kind=kOutput, calls=%fused_computation.9 | convolution fusion | flops 1075314688 | bytes 5242880 | tf_op jit(solution)/shard_map/dot_general | solution.py:27
  (36 shorter events, 0.5 us)
Async XLA Ops:
  7.2 78.5 %copy-start = (bf16[1024,1024]{1,0:T(8,128)(2,1)S(1)}, bf16[1024,1024]{1,0:T(8,128)(2,1)}, u32[]{:S(2)}) copy-start(bf16[1024,1024]{1,0:T(8,128)(2,1)} %param.9) | copy-start | bytes 6291460
  12.4 26.5 %copy-start.2 = (bf16[512,128]{1,0:T(8,128)(2,1)S(1)}, bf16[512,128]{1,0:T(8,128)(2,1)}, u32[]{:S(2)}) copy-start(bf16[512,128]{1,0:T(8,128)(2,1)} %param.15) | copy-start | bytes 393220
  16.8 41.7 %copy-start.1 = (bf16[512,1024]{1,0:T(8,128)(2,1)S(1)}, bf16[512,1024]{1,0:T(8,128)(2,1)}, u32[]{:S(2)}) copy-start(bf16[512,1024]{1,0:T(8,128)(2,1)} %param.8) | copy-start | bytes 3145732
  20.0 33.1 %all-to-all-start = ((s32[64,1,10]{2,1,0:T(1,128)}), s32[64,1,10]{2,1,0:T(1,128)S(1)}, u32[]{:S(2)}, u32[]{:S(2)}) async-start(s32[64,1,10]{2,1,0:T(1,128)} %bitcast.6), calls=%async_computation.1 | async-start | bytes 65536 | tf_op jit(solution)/shard_map/all_to_all | solution.py:58
  53.1 25.8 %all-to-all-start.3 = ((bf16[64,10,128]{2,1,0:T(8,128)(2,1)}), bf16[64,10,128]{2,1,0:T(8,128)(2,1)S(1)}, u32[]{:S(2)}, u32[]{:S(2)}) async-start(bf16[64,10,128]{2,1,0:T(8,128)(2,1)} %broadcast_select_fusion.1), calls=%async_computation.4 | async-start | bytes 524288 | tf_op jit(solution)/shard_map/all_to_all | solution.py:57
  78.9 103.7 %all-to-all-start.1 = ((bf16[64,10,1024]{2,1,0:T(8,128)(2,1)}), bf16[64,10,1024]{2,1,0:T(8,128)(2,1)}, u32[]{:S(2)}, u32[]{:S(2)}) async-start(bf16[64,10,1024]{2,1,0:T(8,128)(2,1)} %broadcast_select_fusion), calls=%async_computation.2 | async-start | bytes 4194304 | tf_op jit(solution)/shard_map/all_to_all | solution.py:56
  85.6 173.3 %reduce-scatter.2.cloned.1.call-start = ((), (), s32[]{:S(2)}) async-start(), calls=%async_computation.6 | async-start | bytes 2359296 | tf_op jit(solution)/shard_map/reduce_scatter | solution.py:18
  88.4 1.5 copy-start.5
  89.9 0.9 copy-start.3
  211.2 10.6 %copy-start.4 = (bf16[640,64]{0,1:T(8,128)(2,1)}, bf16[640,64]{0,1:T(8,128)(2,1)S(1)}, u32[]{:S(2)}) copy-start(bf16[640,64]{0,1:T(8,128)(2,1)S(1)} %get-tuple-element.20) | copy-start | bytes 245764
  212.2 31.2 %all-to-all-start.2 = ((bf16[64,10,128]{2,1,0:T(8,128)(2,1)}), bf16[64,10,128]{2,1,0:T(8,128)(2,1)}, u32[]{:S(2)}, u32[]{:S(2)}) async-start(bf16[64,10,128]{2,1,0:T(8,128)(2,1)} %reshape.164), calls=%async_computation.3 | async-start | bytes 524288 | tf_op jit(solution)/shard_map/all_to_all | solution.py:120
  224.9 26.1 %copy-start.6 = (s32[2]{0:T(128)S(1)}, s32[2]{0:T(128)}, u32[]{:S(2)}) copy-start(s32[2]{0:T(128)} %param.14) | copy-start | bytes 28
  243.4 104.6 %all-to-all-start.4 = ((bf16[64,10,1024]{2,1,0:T(8,128)(2,1)}), bf16[64,10,1024]{2,1,0:T(8,128)(2,1)}, u32[]{:S(2)}, u32[]{:S(2)}) async-start(bf16[64,10,1024]{2,1,0:T(8,128)(2,1)} %reshape.167), calls=%async_computation.5 | async-start | bytes 4194304 | tf_op jit(solution)/shard_map/all_to_all | solution.py:121
  250.3 103.2 %all-gather.2.cloned.1.call-start = ((), (), s32[]{:S(2)}) async-start(), calls=%async_computation.7 | async-start | bytes 1179648 | tf_op jit(solution)/shard_map/all_gather | solution.py:28
Sparse Core Ops, SparseCore 0:
  89.3 39.5 reduce-scatter.1
  253.2 30.8 all-gather.1
where the time goes:
time: 365 us; the launch traced here: 364 us
  waiting for transfers between devices  218 us (60%)
  starting transfers between devices  47.3 us (13%)
  local copies, waits for them, and re-layouts  37.7 us (10%)
  blocking collectives  24.5 us (7%)
  between operations  14.4 us (4%)
  matrix products  13.4 us (4%)
  other arithmetic  8.32 us (2%)
    all_to_all x1, waiting for transfers between devices, shards(): lax.all_to_all(send_tokens, 'dp', split_axis=0, concat_axis=0, tiled=True)  91.8 us
    all_to_all x1, waiting for transfers between devices, shards(): lax.all_to_all(adapter_gradient, 'dp', split_axis=0, concat_axis=0, tiled...  87.4 us
    psum x1, blocking collectives, shards(): rank_activation, backward_result = lax.psum((inner_part, back_part), 'mp')  24.5 us
    all_to_all x1, starting transfers between devices, shards(): lax.all_to_all(send_panel, 'dp', split_axis=0, concat_axis=0, tiled=True)  18.7 us
    all_to_all x1, waiting for transfers between devices, shards(): lax.all_to_all(adapter_delta, 'dp', split_axis=0, concat_axis=0, tiled=True)  18.6 us
    all_to_all x1, waiting for transfers between devices, shards(): lax.all_to_all(send_upstream, 'dp', split_axis=0, concat_axis=0, tiled=True)  10.2 us
    all_to_all x1, waiting for transfers between devices, shards(): lax.all_to_all(send_panel, 'dp', split_axis=0, concat_axis=0, tiled=True)  9.78 us
    all_to_all x1, starting transfers between devices, shards(): lax.all_to_all(adapter_delta, 'dp', split_axis=0, concat_axis=0, tiled=True)  9.58 us
  transfers between devices with their start and end apart: 7, of which 5 were waited for; matrix products, arithmetic and copies ran while one was open for 12% of the time, Pallas kernels for 0%

commit v1 on v0

v1 whole, which is shorter than its diff:
```python
import jax
import jax.numpy as jnp
from jax import lax
from jax.experimental import pallas as pl
from jax.experimental.pallas import tpu as pltpu
from jax.sharding import Mesh
from jax.sharding import PartitionSpec as P

SCALE = 2.0
F32 = jnp.float32
BF16 = jnp.bfloat16
NY, NZ, NX, NC = 4, 16, 4, 2
NM = NX * NC
PAD = 16
FAR = NZ // 2
DP = ("y", "z")
MP = ("x", "core")
BATCHES = ((0, 9), (9, 13), (13, 16))
CHUNKS = 2 * FAR - 1


def dot(a, b, ca, cb):
    return lax.dot_general(a, b, (((ca,), (cb,)), ((), ())), preferred_element_type=F32)


def below(s):
    return 0 if s == 0 else (NZ - 1 if s == FAR else 2 * s - 1)


def above(s):
    return 0 if s == 0 else (NZ - 1 if s == FAR else 2 * s)


def kernel(packed, send, ret, total, panels, rbuf, rets, pk, rsr, pkf, part, psend, prec,
           ag_s, ag_r, y_s, y_r, rt_s, rt_r, xs_s, xs_r, xg_s, xg_r, rs_s, rs_r, loc):
    feats = packed.shape[1] - 128
    half = packed.shape[0] // 2
    yi, zi, xi, ci = (lax.axis_index(n) for n in ("y", "z", "x", "core"))
    m = xi * NC + ci
    up = {"z": lax.rem(zi + 1, NZ)}
    down = {"z": lax.rem(zi + NZ - 1, NZ)}

    def y_peer(d):
        return {"y": lax.rem(yi + d, NY)}

    def m_peer(d):
        p = lax.rem(m + d, NM)
        return {"x": p // NC, "core": lax.rem(p, NC)}

    bar = pltpu.get_barrier_semaphore()
    peers = [up, down] + [y_peer(d) for d in range(1, NY)] + [m_peer(d) for d in range(1, NM)]
    for p in peers:
        pl.semaphore_signal(bar, inc=1, device_id=p, device_id_type=pl.DeviceIdType.MESH)
    pl.semaphore_wait(bar, len(peers))

    started = []

    def remote(src, dst, ssem, rsem, dev):
        c = pltpu.make_async_remote_copy(
            src_ref=src, dst_ref=dst, send_sem=ssem, recv_sem=rsem, device_id=dev,
            device_id_type=pl.DeviceIdType.MESH,
        )
        return c

    def go(*a):
        c = remote(*a)
        c.start()
        started.append(c)

    def ag_start(c):
        s, h = c // 2, c % 2
        for w, (dev, here, there) in enumerate(
            ((up, below(s), below(s + 1)), (down, above(s), above(s + 1)))
        ):
            hh = h if w == 0 else 1 - h
            rows = pl.ds(half * hh, half)
            src = packed.at[rows] if s == 0 else panels.at[here, rows]
            go(src, panels.at[there, rows], ag_s.at[w, c], ag_r.at[w, c], dev)

    def ag_wait(c):
        s, h = c // 2, c % 2
        for w, (dev, there) in enumerate(((up, below(s + 1)), (down, above(s + 1)))):
            hh = h if w == 0 else 1 - h
            ref = panels.at[there, pl.ds(half * hh, half)]
            remote(ref, ref, ag_s.at[w, c], ag_r.at[w, c], dev).wait_recv()

    ag_start(0)
    ag_start(1)
    mine_rows = pl.ds(pl.multiple_of(yi * PAD, PAD), PAD)
    for d in range(1, NY):
        go(send.at[lax.rem(yi + d, NY)], rbuf.at[:, mine_rows, :], y_s.at[d], y_r.at[d], y_peer(d))
    own = pltpu.make_async_copy(send.at[yi], rbuf.at[:, mine_rows, :], loc.at[0])
    own.start()
    panels[0] = packed[...]

    lane = lax.broadcasted_iota(jnp.int32, (NY * PAD, 128), 1) < 64

    def masks(k):
        v = rbuf[k, :, feats:].astype(F32).reshape(NY, PAD, 128)[:, PAD - 1 :, :]
        return jnp.broadcast_to(v, (NY, PAD, 128)).reshape(NY * PAD, 128)

    def rows_wait():
        own.wait()
        for d in range(1, NY):
            src = rbuf.at[:, pl.ds(pl.multiple_of(lax.rem(yi + NY - d, NY) * PAD, PAD), PAD), :]
            remote(src, src, y_s.at[d], y_r.at[d], y_peer(d)).wait_recv()

    def first(k):
        mask = masks(k)
        inner = dot(rbuf[k, :, :feats], panels[k, :, :feats], 1, 1) * mask
        back = dot(rbuf[k, :, feats:], panels[k, :, feats:], 1, 1) * mask
        inner = inner + pltpu.roll(inner, 64, 1)
        back = back + pltpu.roll(back, 64, 1)
        pk[k] = jnp.where(lane, inner, back)

    def x_send(b):
        k0, k1 = BATCHES[b]
        for d in range(1, NM):
            p = lax.rem(m + d, NM)
            go(pk.at[k0:k1, pl.ds(pl.multiple_of(p * 8, 8), 8), :], rsr.at[m, k0:k1],
               xs_s.at[b, d], xs_r.at[b, d], m_peer(d))

    def x_reduce(b):
        k0, k1 = BATCHES[b]
        mine = pl.ds(pl.multiple_of(m * 8, 8), 8)
        acc = pk[k0:k1, mine, :]
        for d in range(1, NM):
            src = lax.rem(m + NM - d, NM)
            ref = rsr.at[src, k0:k1]
            remote(ref, ref, xs_s.at[b, d], xs_r.at[b, d], m_peer(d)).wait_recv()
            acc = acc + rsr[src, k0:k1]
        pkf[k0:k1, mine, :] = acc.astype(BF16).astype(F32)
        for d in range(1, NM):
            ref = pkf.at[k0:k1, mine, :]
            go(ref, ref, xg_s.at[b, d], xg_r.at[b, d], m_peer(d))

    def x_finish(b):
        k0, k1 = BATCHES[b]
        for d in range(1, NM):
            src = lax.rem(m + NM - d, NM)
            ref = pkf.at[k0:k1, pl.ds(pl.multiple_of(src * 8, 8), 8), :]
            remote(ref, ref, xg_s.at[b, d], xg_r.at[b, d], m_peer(d)).wait_recv()

    def spread(k):
        mask = masks(k)
        v = pkf[k]
        r = pltpu.roll(v, 64, 1)
        return (jnp.where(lane, v, r) * mask).astype(BF16), (jnp.where(lane, r, v) * mask).astype(BF16)

    def sums(k):
        inner, back = spread(k)
        part[k, :, :feats] = dot(back, rbuf[k, :, :feats], 0, 0)
        part[k, :, feats:] = dot(inner, rbuf[k, :, feats:], 0, 0)

    def rows_back(k):
        inner, back = spread(k)
        grad = (SCALE * dot(back, panels[k, :, :feats], 1, 0)).astype(BF16)
        delta = (SCALE * dot(inner, panels[k, :, feats:], 1, 0)).astype(BF16)
        for q in range(NY):
            rets[q, k, :, :feats] = grad[q * PAD : (q + 1) * PAD]
            rets[q, k, :, feats:] = delta[q * PAD : (q + 1) * PAD]

    locals_ = [own]

    def ret_send(i, k0, k1):
        for d in range(1, NY):
            go(rets.at[lax.rem(yi + d, NY), k0:k1], ret.at[yi, k0:k1], rt_s.at[i, d], rt_r.at[i, d], y_peer(d))
        c = pltpu.make_async_copy(rets.at[yi, k0:k1], ret.at[yi, k0:k1], loc.at[1 + i])
        c.start()
        locals_.append(c)

    def ret_wait(i, k0, k1):
        locals_[1 + i].wait()
        for d in range(1, NY):
            ref = ret.at[lax.rem(yi + NY - d, NY), k0:k1]
            remote(ref, ref, rt_s.at[i, d], rt_r.at[i, d], y_peer(d)).wait_recv()

    def ag_step(c):
        ag_wait(c)
        if c + 2 < CHUNKS:
            ag_start(c + 2)

    for c in range(9):
        ag_step(c)
    rows_wait()
    for k in range(3):
        first(k)
    ag_step(9)
    for k in range(3, 6):
        first(k)
    ag_step(10)
    for k in range(6, 9):
        first(k)
    x_send(0)
    ag_step(11)
    first(9)
    first(10)
    x_reduce(0)
    ag_step(12)
    first(11)
    first(12)
    x_send(1)
    x_finish(0)
    rows_back(0)
    ag_step(13)
    first(13)
    first(14)
    x_reduce(1)
    ag_step(14)
    first(15)
    x_send(2)
    x_finish(1)
    for k in range(1, 5):
        rows_back(k)
    x_reduce(2)
    for k in range(5, 8):
        rows_back(k)
    ret_send(0, 0, 8)
    x_finish(2)

    def piece(w, c):
        s, h = FAR - (c + 1) // 2, (c % 2 if c else 0)
        hh = h if w == 0 else 1 - h
        return (above(s) if w == 0 else below(s)), pl.ds(half * hh, half)

    def rs_step(c):
        for w, dev in enumerate((up, down)):
            k, rows = piece(w, c)
            v = part[k, rows, :]
            if c >= 2:
                ref = prec.at[w, c - 2]
                remote(ref, ref, rs_s.at[w, c - 2], rs_r.at[w, c - 2], dev).wait_recv()
                v = v + prec[w, c - 2].astype(F32)
            psend[w, c] = v.astype(BF16)
            go(psend.at[w, c], prec.at[w, c], rs_s.at[w, c], rs_r.at[w, c], dev)

    sums(15)
    rs_step(0)
    sums(14)
    sums(13)
    rs_step(1)
    rows_back(8)
    rows_back(9)
    rs_step(2)
    for i, s in enumerate(range(6, 0, -1)):
        sums(2 * s)
        sums(2 * s - 1)
        rs_step(3 + 2 * i)
        if i < 3:
            rows_back(10 + 2 * i)
            rows_back(11 + 2 * i)
        if i == 2:
            ret_send(1, 8, 16)
        rs_step(4 + 2 * i)
    sums(0)
    ret_wait(0, 0, 8)
    ret_wait(1, 8, 16)
    for w, dev in enumerate((up, down)):
        for c in (CHUNKS - 2, CHUNKS - 1):
            ref = prec.at[w, c]
            remote(ref, ref, rs_s.at[w, c], rs_r.at[w, c], dev).wait_recv()
    first_half = part[0, :half] + prec[0, CHUNKS - 1].astype(F32) + prec[1, CHUNKS - 2].astype(F32)
    second_half = part[0, half:] + prec[0, CHUNKS - 2].astype(F32) + prec[1, CHUNKS - 1].astype(F32)
    total[:half] = first_half
    total[half:] = second_half
    for c in started:
        c.wait_send()


def exchange(packed, send):
    n, wide = packed.shape
    half = n // 2
    vm = pl.BlockSpec(memory_space=pltpu.VMEM)
    dma = pltpu.SemaphoreType.DMA
    rows = NY * PAD
    return pl.pallas_call(
        kernel,
        out_shape=(
            jax.ShapeDtypeStruct((NY, NZ, PAD, wide), BF16),
            jax.ShapeDtypeStruct((n, wide), F32),
        ),
        in_specs=[vm, vm],
        out_specs=(vm, vm),
        scratch_shapes=[
            pltpu.VMEM((NZ, n, wide), BF16),
            pltpu.VMEM((NZ, rows, wide), BF16),
            pltpu.VMEM((NY, NZ, PAD, wide), BF16),
            pltpu.VMEM((NZ, rows, 128), F32),
            pltpu.VMEM((NM, NZ, rows // NM, 128), F32),
            pltpu.VMEM((NZ, rows, 128), F32),
            pltpu.VMEM((NZ, n, wide), F32),
            pltpu.VMEM((2, CHUNKS, half, wide), BF16),
            pltpu.VMEM((2, CHUNKS, half, wide), BF16),
            dma((2, CHUNKS)), dma((2, CHUNKS)),
            dma((NY,)), dma((NY,)),
            dma((2, NY)), dma((2, NY)),
            dma((len(BATCHES), NM)), dma((len(BATCHES), NM)),
            dma((len(BATCHES), NM)), dma((len(BATCHES), NM)),
            dma((2, CHUNKS)), dma((2, CHUNKS)),
            dma((3,)),
        ],
        compiler_params=pltpu.CompilerParams(
            collective_id=0, has_side_effects=True, vmem_limit_bytes=56 * 2**20
        ),
        cost_estimate=pl.CostEstimate(flops=2 * 10**9, bytes_accessed=10**8, transcendentals=0),
    )(packed, send)


def shards(tokens, base_weight, adapter_a, adapter_b, row_ids, panel_of, stop_flags, upstream):
    rows = tokens.shape[0]
    per_owner, feats, rank = adapter_a.shape
    vals = upstream.shape[1]
    n_panels = panel_of.shape[0]
    owners = NY * NZ
    wide = feats + vals
    zi = lax.axis_index("z")
    packed = jnp.concatenate(
        [
            jnp.transpose(adapter_a, (0, 2, 1)).reshape(per_owner * rank, feats),
            adapter_b.reshape(per_owner * rank, vals),
        ],
        axis=1,
    )
    matches = row_ids[:, None] == jnp.arange(n_panels, dtype=jnp.int32)[None, :]
    panel = jnp.sum(jnp.where(matches, panel_of[None, :], 0), axis=1)
    owner = panel // per_owner
    within = panel % per_owner
    t = jnp.arange(rows, dtype=jnp.int32)
    earlier = jnp.sum(
        ((owner[:, None] == owner[None, :]) & (t[:, None] < t[None, :])).astype(jnp.int32), axis=0
    )
    away = (owner % NZ - zi + NZ) % NZ
    order = jnp.where(away == FAR, NZ - 1, jnp.where(away < FAR, 2 * away, 2 * (NZ - away) - 1))
    block = (owner // NZ) * NZ + order
    slot = block * PAD + earlier
    slots = owners * PAD
    place = (slot[None, :] == jnp.arange(slots, dtype=jnp.int32)[:, None]).astype(BF16)
    held = block[None, :] == jnp.arange(owners, dtype=jnp.int32)[:, None]
    which = jnp.max(jnp.where(held, within[None, :], 0), axis=1)
    both = jnp.concatenate([tokens, upstream], axis=1)
    col = jnp.arange(wide, dtype=jnp.int32)
    pick = ((col[None, :] - feats) // rank == which[:, None]) & (col[None, :] >= feats)
    last = jnp.arange(PAD, dtype=jnp.int32) == PAD - 1
    send = dot(place, both, 1, 0).reshape(owners, PAD, wide)
    send = jnp.where(last[None, :, None], pick.astype(F32)[:, None, :], send).astype(BF16)
    send = send.reshape(NY, NZ, PAD, wide)
    frozen_output = lax.psum_scatter(
        dot(base_weight, tokens, 0, 1), MP, scatter_dimension=0, tiled=True
    ).T
    all_up = lax.all_gather(upstream, MP, axis=1, tiled=True)
    frozen_gradient = dot(all_up, base_weight, 1, 1)
    ret, total = exchange(packed, send)
    mine = dot(place, ret.reshape(slots, wide), 0, 0)
    projected = (frozen_output + mine[:, feats:]).astype(BF16)
    token_input_gradient = (frozen_gradient + mine[:, :feats]).astype(BF16)
    active = (1 - stop_flags).astype(F32)
    scale = (SCALE * active)[:, None, None]
    down_gradient = scale * total[:, :feats].reshape(per_owner, rank, feats)
    up_gradient = scale * total[:, feats:].reshape(per_owner, rank, vals)
    return (
        projected,
        token_input_gradient,
        jnp.transpose(down_gradient, (0, 2, 1)).astype(BF16),
        up_gradient.astype(BF16),
    )


def solution(mesh):
    fine = Mesh(mesh.devices.reshape(NY, NZ, NX, NC), ("y", "z", "x", "core"))
    placed = (
        P(DP, MP),
        P(MP, None),
        P(DP, MP, None),
        P(DP, None, MP),
        P(DP),
        P(),
        P(DP),
        P(DP, MP),
    )
    return jax.shard_map(
        shards,
        mesh=fine,
        in_specs=placed,
        out_specs=(P(DP, MP), P(DP, MP), P(DP, MP, None), P(DP, None, MP)),
        check_vma=False,
    )
```

time: 365 us -> 173 us (0.47)
  the two profiles are of different devices: /device:TPU:6 before, /device:TPU:1 now
where the time goes in v1:
time: 173 us; the launch traced here: 172 us
  Pallas kernels  131 us (76%)
  matrix products  14.2 us (8%)
  between operations  14.2 us (8%)
  local copies, waits for them, and re-layouts  5.79 us (3%)
  other arithmetic  5.75 us (3%)
    pallas_call x1, Pallas kernels, exchange(): pl.pallas_call(kernel, out_shape=(jax.ShapeDtypeStruct((NY, NZ, PAD, wide...  131 us
    dot_general x4, matrix products, dot(): lax.dot_general(a, b, (((ca,), (cb,)), ((), ())), preferred_element_type=...  14.2 us
    unnamed x18, local copies, waits for them, and re-layouts  3.76 us
  transfers between devices with their start and end apart: 2, of which 0 were waited for; matrix products, arithmetic and copies ran while one was open for 12% of the time, Pallas kernels for 76%

profile of v1, /device:TPU:1, one launch (start us, length us, event | category | flops | bytes accessed | tf_op | source)
XLA Modules:
  0.0 172.1 jit_solution(10256696182613496744)
XLA Ops:
  7.2 0.0 copy-start
  7.2 0.0 all-gather.2.cloned.1.call-start
  7.2 0.7 all-gather.2.cloned.1.call-update
  7.9 0.0 reduce-scatter.2.cloned.1.call-start
  8.0 0.8 copy-done
  8.8 3.9 %fusion.24 = f32[1024,512]{1,0:T(8,128)} fusion(bf16[1024,1024]{1,0:T(8,128)(2,1)S(1)} %copy-done, bf16[512,1024]{1,0:T(8,128)(2,1)} %param.8), kind=kOutput, calls=%fused_computation.63 | convolution fusion | flops 1073741824 | bytes 5242880 | tf_op jit(solution)/shard_map/dot_general | solution.py:23
  12.7 0.0 copy-start.5
  12.7 0.0 copy-start.6
  12.7 0.0 copy-start.1
  12.7 0.0 copy-start.3
  12.7 0.0 copy-start.2
  12.7 0.0 reduce-scatter.2.cloned.1.call-update
  12.7 0.6 copy-done.5
  13.3 0.0 copy-done.6
  13.3 0.2 select_reduce_fusion
  13.6 0.2 convert_reduce_fusion
  13.8 0.1 select_reduce_fusion.1
  13.9 0.1 eq.107
  14.0 0.0 copy-done.1
  14.0 0.0 copy-done.3
  14.1 0.7 pad_maximum_fusion.packed
  14.8 0.0 copy-done.2
  14.8 2.8 %fusion.2 = bf16[1024,1152]{1,0:T(8,128)(2,1)S(1)} fusion(bf16[512,128]{1,0:T(8,128)(2,1)S(1)} %copy-done.2, bf16[512,1024]{1,0:T(8,128)(2,1)} %param.8, s32[512]{0:T(512)S(1)} %get-tuple-element.16), kind=kOutput, calls=%fused_computation.5 | convolution fusion | flops 1210843136 | bytes 3540992 | tf_op jit(solution)/shard_map/dot_general | solution.py:23
  17.6 0.1 and_convert_fusion
  17.7 1.8 %select_convert_fusion.send = bf16[4,16,16,1152]{3,2,1,0:T(8,128)(2,1)} fusion(bf16[4,16,16,1152]{3,2,1,0:T(8,128)(2,1)S(1)} %bitcast.19, bf16[4,16,1152]{2,1,0:T(8,128)(2,1)S(1)} %and_convert_fusion, pred[16]{0:T(512)(128)(4,1)S(1)} %iota_compare_fusion.7), kind=kLoop, calls=%fused_computation | loop fusion | flops 1179648 | bytes 4866064 | tf_op jit(solution)/shard_map/convert_element_type | solution.py:345
  19.6 131.5 %shard_map.111 = (bf16[4,16,16,1152]{3,2,1,0:T(8,128)(2,1)}, f32[128,1152]{1,0:T(8,128)}) custom-call(bf16[128,1152]{1,0:T(8,128)(2,1)} %pad_maximum_fusion.packed, bf16[4,16,16,1152]{3,2,1,0:T(8,128)(2,1)} %select_convert_fusion.send), custom_call_target="tpu_custom_call" | custom-call | flops 2000000000 | bytes 100000000 | tf_op jit(solution)/shard_map/pallas_call | solution.py:276
  151.0 1.1 slice.14
  152.1 0.8 slice.15
  153.0 0.0 copy-start.7
  153.0 3.3 %fusion.1 = f32[512,1152]{1,0:T(8,128)S(1)} fusion(bf16[1024,1152]{1,0:T(8,128)(2,1)} %bitcast.24, s32[512]{0:T(512)S(1)} %get-tuple-element.16), kind=kOutput, calls=%fused_computation.4 | convolution fusion | flops 1208483840 | bytes 4720640 | tf_op jit(solution)/shard_map/dot_general | solution.py:23
  156.3 0.0 copy-start.4
  156.3 1.4 copy-done.4
  157.7 0.1 copy.16
  157.8 0.0 copy-done.7
  157.8 0.7 multiply_convert_fusion.1
  158.5 0.8 fusion.9
  159.3 0.0 all-gather.2.cloned.1.call-done
  159.4 4.2 %fusion = bf16[512,1024]{1,0:T(8,128)(2,1)} fusion(f32[512,1152]{1,0:T(8,128)} %copy-done.4, bf16[512,1024]{1,0:T(8,128)(2,1)} %all-gather.2.cloned.1.call-done, bf16[1024,1024]{1,0:T(8,128)(2,1)S(1)} %copy-done), kind=kOutput, calls=%fused_computation.2 | convolution fusion | flops 1074790400 | bytes 6291456 | tf_op jit(solution)/shard_map/dot_general | solution.py:23
  163.5 0.0 reduce-scatter.2.cloned.1.call-done
  163.5 1.0 fusion.10
  164.5 0.8 copy.15
  (7 shorter events, 0.1 us)
Async XLA Ops:
  7.2 1.6 copy-start
  7.2 152.2 %all-gather.2.cloned.1.call-start = ((), (), s32[]{:S(2)}) async-start(), calls=%async_computation.2 | async-start | bytes 1179648 | tf_op jit(solution)/shard_map/all_gather | solution.py:350
  7.9 155.6 %reduce-scatter.2.cloned.1.call-start = ((), (), s32[]{:S(2)}) async-start(), calls=%async_computation.1 | async-start | bytes 2359296 | tf_op jit(solution)/shard_map/reduce_scatter | solution.py:347
  12.7 0.7 copy-start.5
  12.7 0.7 copy-start.6
  12.7 1.4 copy-start.1
  12.7 1.4 copy-start.3
  12.7 2.1 %copy-start.2 = (bf16[512,128]{1,0:T(8,128)(2,1)S(1)}, bf16[512,128]{1,0:T(8,128)(2,1)}, u32[]{:S(2)}) copy-start(bf16[512,128]{1,0:T(8,128)(2,1)} %param.15) | copy-start | bytes 393220
  153.0 4.9 %copy-start.7 = (s32[2]{0:T(128)S(1)}, s32[2]{0:T(128)}, u32[]{:S(2)}) copy-start(s32[2]{0:T(128)} %param.14) | copy-start | bytes 28
  156.3 1.4 copy-start.4
Sparse Core Ops, SparseCore 0:
  10.1 36.7 all-gather.1
  49.7 45.2 reduce-scatter.1

commit v2 on v1

v2 whole, which is shorter than its diff:
```python
import jax
import jax.numpy as jnp
from jax import lax
from jax.experimental import pallas as pl
from jax.experimental.pallas import tpu as pltpu
from jax.sharding import Mesh
from jax.sharding import PartitionSpec as P

SCALE = 2.0
F32 = jnp.float32
BF16 = jnp.bfloat16
NY, NZ, NX, NC = 4, 16, 4, 2
NM = NX * NC
PAD = 16
FAR = NZ // 2
DP = ("y", "z")
MP = ("x", "core")
BATCHES = ((0, 9), (9, 13), (13, 16))
CHUNKS = 2 * FAR - 1


def dot(a, b, ca, cb):
    return lax.dot_general(a, b, (((ca,), (cb,)), ((), ())), preferred_element_type=F32)


def below(s):
    return 0 if s == 0 else (NZ - 1 if s == FAR else 2 * s - 1)


def above(s):
    return 0 if s == 0 else (NZ - 1 if s == FAR else 2 * s)


def kernel(tok_hbm, w_hbm, at_ref, b_ref, ids_ref, panel_ref, flags_ref, up_ref,
           proj_ref, tig_ref, down_ref, upg_ref,
           tok, w, ua, fs, fr, fg, back_place, send, ret, panels, rbuf, rets, pk, rsr, pkf, part, psend, prec,
           ag_s, ag_r, y_s, y_r, rt_s, rt_r, xs_s, xs_r, xg_s, xg_r, rs_s, rs_r, u_s, u_r, f_s, f_r, loc):
    scope = jax.named_scope
    rows, feats = tok.shape
    wide = feats + 128
    half = at_ref.shape[0] // 2
    yi, zi, xi, ci = (lax.axis_index(n) for n in ("y", "z", "x", "core"))
    m = xi * NC + ci
    up = {"z": lax.rem(zi + 1, NZ)}
    down = {"z": lax.rem(zi + NZ - 1, NZ)}

    def y_peer(d):
        return {"y": lax.rem(yi + d, NY)}

    def m_peer(d):
        p = lax.rem(m + d, NM)
        return {"x": p // NC, "core": lax.rem(p, NC)}

    def lanes(p):
        return pl.ds(pl.multiple_of(p * 128, 128), 128)

    tok_in = pltpu.make_async_copy(tok_hbm, tok, loc.at[3])
    tok_in.start()
    w_in = pltpu.make_async_copy(w_hbm, w, loc.at[4])
    w_in.start()
    with scope("entry"):
        bar = pltpu.get_barrier_semaphore()
        peers = [up, down] + [y_peer(d) for d in range(1, NY)] + [m_peer(d) for d in range(1, NM)]
        for p in peers:
            pl.semaphore_signal(bar, inc=1, device_id=p, device_id_type=pl.DeviceIdType.MESH)
        panels[0, :, :feats] = at_ref[...]
        panels[0, :, feats:] = b_ref[...]
        pl.semaphore_wait(bar, len(peers))

    started = []

    def remote(src, dst, ssem, rsem, dev):
        return pltpu.make_async_remote_copy(
            src_ref=src, dst_ref=dst, send_sem=ssem, recv_sem=rsem, device_id=dev,
            device_id_type=pl.DeviceIdType.MESH,
        )

    def go(*a):
        c = remote(*a)
        c.start()
        started.append(c)

    def ag_start(c):
        s, h = c // 2, c % 2
        for v, (dev, here, there) in enumerate(
            ((up, below(s), below(s + 1)), (down, above(s), above(s + 1)))
        ):
            part_rows = pl.ds(half * (h if v == 0 else 1 - h), half)
            go(panels.at[here, part_rows], panels.at[there, part_rows], ag_s.at[v, c], ag_r.at[v, c], dev)

    def ag_step(c):
        s, h = c // 2, c % 2
        with scope(f"panel_hop_{c}"):
            for v, (dev, there) in enumerate(((up, below(s + 1)), (down, above(s + 1)))):
                ref = panels.at[there, pl.ds(half * (h if v == 0 else 1 - h), half)]
                remote(ref, ref, ag_s.at[v, c], ag_r.at[v, c], dev).wait_recv()
            if c + 2 < CHUNKS:
                ag_start(c + 2)

    ag_start(0)
    ag_start(1)

    def iota(shape, d):
        return lax.broadcasted_iota(jnp.int32, shape, d)

    def hot(cond):
        return jnp.where(cond, 1.0, 0.0)

    with scope("routing"):
        n_panels = panel_ref.shape[1]
        owners = NY * NZ
        rank = 64
        named = hot(iota((n_panels, rows), 0) == ids_ref[...]).astype(BF16)
        mapped = hot(iota((n_panels, n_panels), 0) == panel_ref[...]).astype(BF16)
        panel_hot = dot(mapped, named, 1, 0)
        panel = jnp.sum(panel_hot * iota((n_panels, rows), 0).astype(F32), axis=0, keepdims=True).astype(jnp.int32)
        owner = panel // 2
        within = panel - owner * 2
        own_y = owner // NZ
        away = owner - own_y * NZ - zi
        away = jnp.where(away < 0, away + NZ, away)
        order = jnp.where(away == FAR, NZ - 1, jnp.where(away < FAR, 2 * away, 2 * (NZ - away) - 1))
        block = own_y * NZ + order
        block_hot = hot(iota((owners, rows), 0) == block)
        before = hot(iota((rows, rows), 0) < iota((rows, rows), 1)).astype(BF16)
        counts = dot(block_hot.astype(BF16), before, 1, 0) * block_hot
        earlier = jnp.sum(counts, axis=0, keepdims=True).astype(jnp.int32)
        slot = block * PAD + earlier
        which = jnp.max(block_hot * within.astype(F32), axis=1, keepdims=True)
        pick = hot((iota((owners, 128), 1) // rank).astype(F32) == which)
        last = iota((NZ * PAD, 128), 0) % PAD == PAD - 1
        tok_in.wait()
    with scope("rows_out"):
        for q in range(NY):
            place = hot(iota((NZ * PAD, rows), 0) + q * NZ * PAD == slot).astype(BF16)
            t = dot(place, tok[...], 1, 0).astype(BF16)
            u = dot(place, up_ref[...], 1, 0)
            marks = jnp.broadcast_to(pick[q * NZ : (q + 1) * NZ].reshape(NZ, 1, 128), (NZ, PAD, 128))
            u = jnp.where(last, marks.reshape(NZ * PAD, 128), u).astype(BF16)
            send[q, :, :, :feats] = t.reshape(NZ, PAD, feats)
            send[q, :, :, feats:] = u.reshape(NZ, PAD, 128)
        mine_rows = pl.ds(pl.multiple_of(yi * PAD, PAD), PAD)
        for d in range(1, NY):
            go(send.at[lax.rem(yi + d, NY)], rbuf.at[:, mine_rows, :], y_s.at[d], y_r.at[d], y_peer(d))
        own = pltpu.make_async_copy(send.at[yi], rbuf.at[:, mine_rows, :], loc.at[0])
        own.start()
    ag_step(0)
    with scope("cotangents_out"):
        for d in range(1, NM):
            go(up_ref, ua.at[:, lanes(m)], u_s.at[d], u_r.at[d], m_peer(d))
        ua[:, lanes(m)] = up_ref[...]
        w_in.wait()
    with scope("base"):
        for j in range(NM // 2):
            r = dot(tok[...], w[:, 256 * j : 256 * j + 256], 1, 0)
            fs[2 * j] = r[:, :128]
            fs[2 * j + 1] = r[:, 128:]
    ag_step(1)
    with scope("base_out"):
        for d in range(1, NM):
            p = lax.rem(m + d, NM)
            go(fs.at[p], fr.at[m], f_s.at[d], f_r.at[d], m_peer(d))
    ag_step(2)
    with scope("row_places"):
        ones = jnp.ones((owners, 128), BF16)
        blocks = dot((block_hot * iota((owners, rows), 0).astype(F32)).astype(BF16), ones, 0, 0)
        slot_col = blocks * PAD + dot(counts.astype(BF16), ones, 0, 0)
        for j in range(owners * PAD // 128):
            back_place[:, 128 * j : 128 * j + 128] = hot(
                (iota((rows, 128), 1) + 128 * j).astype(F32) == slot_col
            ).astype(BF16)
    ag_step(3)
    with scope("cotangents_wait"):
        for d in range(1, NM):
            ref = ua.at[:, lanes(lax.rem(m + NM - d, NM))]
            remote(ref, ref, u_s.at[d], u_r.at[d], m_peer(d)).wait_recv()
    ag_step(4)
    with scope("base_gradient"):
        for j in range(2):
            fg[256 * j : 256 * j + 256] = dot(ua[256 * j : 256 * j + 256], w[...], 1, 1)
    ag_step(5)

    lane = iota((NY * PAD, 128), 1) < 64

    def masks(k):
        v = rbuf[k, :, feats:].astype(F32).reshape(NY, PAD, 128)[:, PAD - 1 :, :]
        return jnp.broadcast_to(v, (NY, PAD, 128)).reshape(NY * PAD, 128)

    def rows_wait():
        with scope("rows_wait"):
            own.wait()
            for d in range(1, NY):
                ref = rbuf.at[:, pl.ds(pl.multiple_of(lax.rem(yi + NY - d, NY) * PAD, PAD), PAD), :]
                remote(ref, ref, y_s.at[d], y_r.at[d], y_peer(d)).wait_recv()

    def first(k):
        mask = masks(k)
        inner = dot(rbuf[k, :, :feats], panels[k, :, :feats], 1, 1) * mask
        back = dot(rbuf[k, :, feats:], panels[k, :, feats:], 1, 1) * mask
        inner = inner + pltpu.roll(inner, 64, 1)
        back = back + pltpu.roll(back, 64, 1)
        pk[k] = jnp.where(lane, inner, back)

    def x_send(b):
        k0, k1 = BATCHES[b]
        for d in range(1, NM):
            p = lax.rem(m + d, NM)
            go(pk.at[k0:k1, pl.ds(pl.multiple_of(p * 8, 8), 8), :], rsr.at[m, k0:k1],
               xs_s.at[b, d], xs_r.at[b, d], m_peer(d))

    def x_reduce(b):
        k0, k1 = BATCHES[b]
        mine = pl.ds(pl.multiple_of(m * 8, 8), 8)
        acc = pk[k0:k1, mine, :]
        for d in range(1, NM):
            src = lax.rem(m + NM - d, NM)
            ref = rsr.at[src, k0:k1]
            remote(ref, ref, xs_s.at[b, d], xs_r.at[b, d], m_peer(d)).wait_recv()
            acc = acc + rsr[src, k0:k1]
        pkf[k0:k1, mine, :] = acc.astype(BF16).astype(F32)
        for d in range(1, NM):
            ref = pkf.at[k0:k1, mine, :]
            go(ref, ref, xg_s.at[b, d], xg_r.at[b, d], m_peer(d))

    def x_finish(b):
        k0, k1 = BATCHES[b]
        for d in range(1, NM):
            src = lax.rem(m + NM - d, NM)
            ref = pkf.at[k0:k1, pl.ds(pl.multiple_of(src * 8, 8), 8), :]
            remote(ref, ref, xg_s.at[b, d], xg_r.at[b, d], m_peer(d)).wait_recv()

    def spread(k):
        mask = masks(k)
        v = pkf[k]
        r = pltpu.roll(v, 64, 1)
        return (jnp.where(lane, v, r) * mask).astype(BF16), (jnp.where(lane, r, v) * mask).astype(BF16)

    def sums(k):
        inner, back = spread(k)
        part[k, :, :feats] = dot(back, rbuf[k, :, :feats], 0, 0)
        part[k, :, feats:] = dot(inner, rbuf[k, :, feats:], 0, 0)

    def rows_back(k):
        inner, back = spread(k)
        grad = (SCALE * dot(back, panels[k, :, :feats], 1, 0)).astype(BF16)
        delta = (SCALE * dot(inner, panels[k, :, feats:], 1, 0)).astype(BF16)
        for q in range(NY):
            rets[q, k, :, :feats] = grad[q * PAD : (q + 1) * PAD]
            rets[q, k, :, feats:] = delta[q * PAD : (q + 1) * PAD]

    locals_ = [own]

    def ret_send(i, k0, k1):
        for d in range(1, NY):
            go(rets.at[lax.rem(yi + d, NY), k0:k1], ret.at[yi, k0:k1], rt_s.at[i, d], rt_r.at[i, d], y_peer(d))
        c = pltpu.make_async_copy(rets.at[yi, k0:k1], ret.at[yi, k0:k1], loc.at[1 + i])
        c.start()
        locals_.append(c)

    def ret_wait(i, k0, k1):
        locals_[1 + i].wait()
        for d in range(1, NY):
            ref = ret.at[lax.rem(yi + NY - d, NY), k0:k1]
            remote(ref, ref, rt_s.at[i, d], rt_r.at[i, d], y_peer(d)).wait_recv()

    for c in range(6, 9):
        ag_step(c)
    rows_wait()
    with scope("ranks_0"):
        for k in range(3):
            first(k)
    ag_step(9)
    with scope("ranks_1"):
        for k in range(3, 6):
            first(k)
    ag_step(10)
    with scope("ranks_2"):
        for k in range(6, 9):
            first(k)
        x_send(0)
    ag_step(11)
    with scope("ranks_3"):
        first(9)
        first(10)
    with scope("reduce_0"):
        x_reduce(0)
    ag_step(12)
    with scope("ranks_4"):
        first(11)
        first(12)
        x_send(1)
    with scope("finish_0"):
        x_finish(0)
    rows_back(0)
    ag_step(13)
    with scope("ranks_5"):
        first(13)
        first(14)
    with scope("reduce_1"):
        x_reduce(1)
    ag_step(14)
    with scope("ranks_6"):
        first(15)
        x_send(2)
    with scope("finish_1"):
        x_finish(1)
    with scope("rows_back_a"):
        for k in range(1, 5):
            rows_back(k)
    with scope("reduce_2"):
        x_reduce(2)
    with scope("rows_back_b"):
        for k in range(5, 8):
            rows_back(k)
        ret_send(0, 0, 8)
    with scope("finish_2"):
        x_finish(2)

    def piece(w, c):
        s, h = FAR - (c + 1) // 2, (c % 2 if c else 0)
        hh = h if w == 0 else 1 - h
        return (above(s) if w == 0 else below(s)), pl.ds(half * hh, half)

    def rs_step(c):
        with scope(f"sum_hop_{c}"):
            for v, dev in enumerate((up, down)):
                k, part_rows = piece(v, c)
                x = part[k, part_rows, :]
                if c >= 2:
                    ref = prec.at[v, c - 2]
                    remote(ref, ref, rs_s.at[v, c - 2], rs_r.at[v, c - 2], dev).wait_recv()
                    x = x + prec[v, c - 2].astype(F32)
                psend[v, c] = x.astype(BF16)
                go(psend.at[v, c], prec.at[v, c], rs_s.at[v, c], rs_r.at[v, c], dev)

    sums(15)
    rs_step(0)
    sums(14)
    sums(13)
    rs_step(1)
    rows_back(8)
    rows_back(9)
    rs_step(2)
    for i, s in enumerate(range(6, 0, -1)):
        with scope("sums"):
            sums(2 * s)
            sums(2 * s - 1)
        rs_step(3 + 2 * i)
        if i < 3:
            with scope("rows_back_c"):
                rows_back(10 + 2 * i)
                rows_back(11 + 2 * i)
        if i == 2:
            ret_send(1, 8, 16)
        if i == 3:
            with scope("base_wait"):
                acc = fs[m]
                for d in range(1, NM):
                    src = lax.rem(m + NM - d, NM)
                    remote(fr.at[src], fr.at[src], f_s.at[d], f_r.at[d], m_peer(d)).wait_recv()
                    acc = acc + fr[src]
                fs[m] = acc
        rs_step(4 + 2 * i)
    sums(0)
    with scope("returned_wait"):
        ret_wait(0, 0, 8)
        ret_wait(1, 8, 16)
    with scope("outputs"):
        mine = ret[...].reshape(NY * NZ * PAD, wide)
        for j in range(4):
            r = pl.ds(128 * j, 128)
            place = back_place[r]
            tig_ref[r] = (fg[r] + dot(place, mine[:, :feats], 1, 0)).astype(BF16)
            proj_ref[r] = (fs[m, r] + dot(place, mine[:, feats:], 1, 0)).astype(BF16)
    with scope("last_sums"):
        for v, dev in enumerate((up, down)):
            for c in (CHUNKS - 2, CHUNKS - 1):
                ref = prec.at[v, c]
                remote(ref, ref, rs_s.at[v, c], rs_r.at[v, c], dev).wait_recv()
        for p in range(2):
            scale = SCALE * (1 - flags_ref[p]).astype(F32)
            c0, c1 = (CHUNKS - 1, CHUNKS - 2) if p == 0 else (CHUNKS - 2, CHUNKS - 1)
            r = slice(p * half, (p + 1) * half)
            v = scale * (part[0, r] + prec[0, c0].astype(F32) + prec[1, c1].astype(F32))
            down_ref[r] = v[:, :feats].astype(BF16)
            upg_ref[r] = v[:, feats:].astype(BF16)
    with scope("sent"):
        for c in started:
            c.wait_send()


def fused(tokens, weight, at, b, ids, panel_of, flags, upstream):
    rows, feats = tokens.shape
    n = at.shape[0]
    half = n // 2
    wide = feats + 128
    vm = pl.BlockSpec(memory_space=pltpu.VMEM)
    hbm = pl.BlockSpec(memory_space=pl.ANY)
    dma = pltpu.SemaphoreType.DMA
    group = NY * PAD
    nb = len(BATCHES)
    return pl.pallas_call(
        kernel,
        out_shape=(
            jax.ShapeDtypeStruct((rows, 128), BF16),
            jax.ShapeDtypeStruct((rows, feats), BF16),
            jax.ShapeDtypeStruct((n, feats), BF16),
            jax.ShapeDtypeStruct((n, 128), BF16),
        ),
        in_specs=[hbm, hbm, vm, vm, vm, vm, pl.BlockSpec(memory_space=pltpu.SMEM), vm],
        out_specs=(vm, vm, vm, vm),
        scratch_shapes=[
            pltpu.VMEM((rows, feats), BF16),
            pltpu.VMEM(weight.shape, BF16),
            pltpu.VMEM((rows, NM * 128), BF16),
            pltpu.VMEM((NM, rows, 128), F32),
            pltpu.VMEM((NM, rows, 128), F32),
            pltpu.VMEM((rows, feats), F32),
            pltpu.VMEM((rows, NY * NZ * PAD), BF16),
            pltpu.VMEM((NY, NZ, PAD, wide), BF16),
            pltpu.VMEM((NY, NZ, PAD, wide), BF16),
            pltpu.VMEM((NZ, n, wide), BF16),
            pltpu.VMEM((NZ, group, wide), BF16),
            pltpu.VMEM((NY, NZ, PAD, wide), BF16),
            pltpu.VMEM((NZ, group, 128), F32),
            pltpu.VMEM((NM, NZ, group // NM, 128), F32),
            pltpu.VMEM((NZ, group, 128), F32),
            pltpu.VMEM((NZ, n, wide), F32),
            pltpu.VMEM((2, CHUNKS, half, wide), BF16),
            pltpu.VMEM((2, CHUNKS, half, wide), BF16),
            dma((2, CHUNKS)), dma((2, CHUNKS)),
            dma((NY,)), dma((NY,)),
            dma((2, NY)), dma((2, NY)),
            dma((nb, NM)), dma((nb, NM)),
            dma((nb, NM)), dma((nb, NM)),
            dma((2, CHUNKS)), dma((2, CHUNKS)),
            dma((NM,)), dma((NM,)),
            dma((NM,)), dma((NM,)),
            dma((5,)),
        ],
        compiler_params=pltpu.CompilerParams(
            collective_id=0, has_side_effects=True, vmem_limit_bytes=58 * 2**20
        ),
        cost_estimate=pl.CostEstimate(flops=5 * 10**9, bytes_accessed=10**7, transcendentals=0),
    )(tokens, weight, at, b, ids, panel_of, flags, upstream)


def shards(tokens, base_weight, adapter_a, adapter_b, row_ids, panel_of, stop_flags, upstream):
    per_owner, feats, rank = adapter_a.shape
    vals = upstream.shape[1]
    at = jnp.transpose(adapter_a, (0, 2, 1)).reshape(per_owner * rank, feats)
    b = adapter_b.reshape(per_owner * rank, vals)
    projected, gradient, down, up = fused(
        tokens, base_weight, at, b, row_ids.reshape(1, -1), panel_of.reshape(1, -1), stop_flags, upstream
    )
    return (
        projected,
        gradient,
        jnp.transpose(down.reshape(per_owner, rank, feats), (0, 2, 1)),
        up.reshape(per_owner, rank, vals),
    )


def solution(mesh):
    fine = Mesh(mesh.devices.reshape(NY, NZ, NX, NC), ("y", "z", "x", "core"))
    placed = (
        P(DP, MP),
        P(MP, None),
        P(DP, MP, None),
        P(DP, None, MP),
        P(DP),
        P(),
        P(DP),
        P(DP, MP),
    )
    return jax.shard_map(
        shards,
        mesh=fine,
        in_specs=placed,
        out_specs=(P(DP, MP), P(DP, MP), P(DP, MP, None), P(DP, None, MP)),
        check_vma=False,
    )
```

time: 173 us -> 138 us (0.80)
  matrix products: 14.2 us -> 0 us
  between operations: 14.2 us -> 0.66 us
  other arithmetic: 5.75 us -> 0 us
    dot_general x4 -> x0, matrix products: 14.2 us -> none  [dot(): lax.dot_general(a, b, (((ca,), (cb,)), ((), ())), preferred_element_type=...]
    convert_element_type x5 -> x0, other arithmetic: 4.42 us -> none  [the longest x1 1.82 us: shards(): jnp.where(last[None, :, None], pick.astype(F32)[:, None, :], send)]
    slice x3 -> x0, local copies, waits for them, and re-layouts: 1.94 us -> none  [the longest x1 1.08 us: shards(): down_gradient = scale * total[:, :feats].reshape(per_owner, rank, feats)]
    unnamed x18 -> x8, local copies, waits for them, and re-layouts: 3.76 us -> 5.2 us
  transfers between devices with their start and end apart: 2 -> 0, of which waited for: 0 -> 0; matrix products, arithmetic and copies ran while one was open for 12% -> 0% of each run, Pallas kernels for 76% -> 0%
where the time goes in v2:
time: 138 us
  Pallas kernels  132 us (96%)
  local copies, waits for them, and re-layouts  5.2 us (4%)
    pallas_call x1, Pallas kernels, fused(): pl.pallas_call(kernel, out_shape=(jax.ShapeDtypeStruct((rows, 128), BF16)...  132 us
    unnamed x8, local copies, waits for them, and re-layouts  5.2 us

profile of v2, /device:TPU:1, one launch (start us, length us, event | category | flops | bytes accessed | tf_op | source)
XLA Modules:
  0.0 137.9 jit_solution(3767041171129366608)
XLA Ops:
  0.6 132.0 %shard_map.111 = (bf16[512,128]{1,0:T(8,128)(2,1)}, bf16[512,1024]{1,0:T(8,128)(2,1)}, bf16[128,1024]{1,0:T(8,128)(2,1)}, bf16[128,128]{1,0:T(8,128)(2,1)}) custom-call(bf16[512,1024]{1,0:T(8,128)(2,1)} %tok_hbm.1, bf16[1024,1024]{1,0:T(8,128)(2,1)} %w_hbm.1, bf16[128,1024]{1,0:T(8,128)(2,1)} %bitcast.12, bf16[128,128]{1,0:T(8,128)(2,1)} %bitcast.13, ...), custom_call_target="tpu_custom_call" | custom-call | flops 5000000000 | bytes 10000000 | tf_op jit(solution)/shard_map/pallas_call | solution.py:402
  132.7 0.0 copy-start
  132.7 0.0 copy-start.1
  132.7 1.6 %copy.16 = bf16[512,128]{1,0:T(8,128)(2,1)} copy(bf16[512,128]{1,0:T(8,128)(2,1)} %get-tuple-element.16) | data formatting | bytes 262144
  134.3 2.3 %copy.17 = bf16[512,1024]{1,0:T(8,128)(2,1)} copy(bf16[512,1024]{1,0:T(8,128)(2,1)} %get-tuple-element.17) | data formatting | bytes 2097152
  136.6 0.0 copy-done
  136.6 0.7 copy.18
  137.3 0.0 copy-done.1
  137.3 0.6 copy.19
Async XLA Ops:
  132.7 3.9 %copy-start = (bf16[128,1024]{1,0:T(8,128)(2,1)S(1)}, bf16[128,1024]{1,0:T(8,128)(2,1)}, u32[]{:S(2)}) copy-start(bf16[128,1024]{1,0:T(8,128)(2,1)} %get-tuple-element.10) | copy-start | bytes 786436
  132.7 4.6 %copy-start.1 = (bf16[128,128]{1,0:T(8,128)(2,1)S(1)}, bf16[128,128]{1,0:T(8,128)(2,1)}, u32[]{:S(2)}) copy-start(bf16[128,128]{1,0:T(8,128)(2,1)} %get-tuple-element.11) | copy-start | bytes 98308

commit v3 on v2

--- a/solution.py
+++ b/solution.py
@@ -15,7 +15,7 @@
 FAR = NZ // 2
 DP = ("y", "z")
 MP = ("x", "core")
-BATCHES = ((0, 9), (9, 13), (13, 16))
+BATCHES = ((0, 9), (9, 13), (13, 15))
 CHUNKS = 2 * FAR - 1
 
 
@@ -33,8 +33,8 @@
 
 def kernel(tok_hbm, w_hbm, at_ref, b_ref, ids_ref, panel_ref, flags_ref, up_ref,
            proj_ref, tig_ref, down_ref, upg_ref,
-           tok, w, ua, fs, fr, fg, back_place, send, ret, panels, rbuf, rets, pk, rsr, pkf, part, psend, prec,
-           ag_s, ag_r, y_s, y_r, rt_s, rt_r, xs_s, xs_r, xg_s, xg_r, rs_s, rs_r, u_s, u_r, f_s, f_r, loc):
+           tok, w, ua, fs, fr, fg, back_place, send, ret, panels, rbuf, rets, pk, rsr, pkf, whole, proj, part, psend, prec,
+           ag_s, ag_r, y_s, y_r, rt_s, rt_r, xs_s, xs_r, xg_s, xg_r, rs_s, rs_r, u_s, u_r, f_s, f_r, b_s, b_r, loc):
     scope = jax.named_scope
     rows, feats = tok.shape
     wide = feats + 128
@@ -296,25 +296,25 @@
     with scope("ranks_5"):
         first(13)
         first(14)
+        x_send(2)
     with scope("reduce_1"):
         x_reduce(1)
     ag_step(14)
     with scope("ranks_6"):
         first(15)
-        x_send(2)
-    with scope("finish_1"):
-        x_finish(1)
+        for d in range(1, NM):
+            go(pk.at[15], whole.at[m], b_s.at[d], b_r.at[d], m_peer(d))
+        whole[m] = pk[15]
+    with scope("reduce_2"):
+        x_reduce(2)
     with scope("rows_back_a"):
         for k in range(1, 5):
             rows_back(k)
-    with scope("reduce_2"):
-        x_reduce(2)
-    with scope("rows_back_b"):
-        for k in range(5, 8):
-            rows_back(k)
-        ret_send(0, 0, 8)
-    with scope("finish_2"):
-        x_finish(2)
+    with scope("finish_last"):
+        for d in range(1, NM):
+            ref = whole.at[lax.rem(m + NM - d, NM)]
+            remote(ref, ref, b_s.at[d], b_r.at[d], m_peer(d)).wait_recv()
+        pkf[15] = sum(whole[j] for j in range(NM)).astype(BF16).astype(F32)
 
     def piece(w, c):
         s, h = FAR - (c + 1) // 2, (c % 2 if c else 0)
@@ -335,24 +335,30 @@
 
     sums(15)
     rs_step(0)
+    with scope("finish_2"):
+        x_finish(2)
     sums(14)
     sums(13)
     rs_step(1)
-    rows_back(8)
-    rows_back(9)
+    with scope("finish_1"):
+        x_finish(1)
+    with scope("rows_back_b"):
+        for k in range(5, 8):
+            rows_back(k)
+        ret_send(0, 0, 8)
     rs_step(2)
     for i, s in enumerate(range(6, 0, -1)):
         with scope("sums"):
             sums(2 * s)
             sums(2 * s - 1)
         rs_step(3 + 2 * i)
-        if i < 3:
+        if i < 4:
             with scope("rows_back_c"):
-                rows_back(10 + 2 * i)
-                rows_back(11 + 2 * i)
-        if i == 2:
+                rows_back(8 + 2 * i)
+                rows_back(9 + 2 * i)
+        if i == 3:
             ret_send(1, 8, 16)
-        if i == 3:
+        if i == 4:
             with scope("base_wait"):
                 acc = fs[m]
                 for d in range(1, NM):
@@ -370,8 +376,12 @@
         for j in range(4):
             r = pl.ds(128 * j, 128)
             place = back_place[r]
-            tig_ref[r] = (fg[r] + dot(place, mine[:, :feats], 1, 0)).astype(BF16)
-            proj_ref[r] = (fs[m, r] + dot(place, mine[:, feats:], 1, 0)).astype(BF16)
+            ua[r] = (fg[r] + dot(place, mine[:, :feats], 1, 0)).astype(BF16)
+            proj[r] = (fs[m, r] + dot(place, mine[:, feats:], 1, 0)).astype(BF16)
+        tig_out = pltpu.make_async_copy(ua, tig_ref, loc.at[5])
+        proj_out = pltpu.make_async_copy(proj, proj_ref, loc.at[6])
+        tig_out.start()
+        proj_out.start()
     with scope("last_sums"):
         for v, dev in enumerate((up, down)):
             for c in (CHUNKS - 2, CHUNKS - 1):
@@ -385,6 +395,8 @@
             down_ref[r] = v[:, :feats].astype(BF16)
             upg_ref[r] = v[:, feats:].astype(BF16)
     with scope("sent"):
+        tig_out.wait()
+        proj_out.wait()
         for c in started:
             c.wait_send()
 
@@ -408,7 +420,7 @@
             jax.ShapeDtypeStruct((n, 128), BF16),
         ),
         in_specs=[hbm, hbm, vm, vm, vm, vm, pl.BlockSpec(memory_space=pltpu.SMEM), vm],
-        out_specs=(vm, vm, vm, vm),
+        out_specs=(hbm, hbm, vm, vm),
         scratch_shapes=[
             pltpu.VMEM((rows, feats), BF16),
             pltpu.VMEM(weight.shape, BF16),
@@ -425,6 +437,8 @@
             pltpu.VMEM((NZ, group, 128), F32),
             pltpu.VMEM((NM, NZ, group // NM, 128), F32),
             pltpu.VMEM((NZ, group, 128), F32),
+            pltpu.VMEM((NM, group, 128), F32),
+            pltpu.VMEM((rows, 128), BF16),
             pltpu.VMEM((NZ, n, wide), F32),
             pltpu.VMEM((2, CHUNKS, half, wide), BF16),
             pltpu.VMEM((2, CHUNKS, half, wide), BF16),
@@ -436,7 +450,8 @@
             dma((2, CHUNKS)), dma((2, CHUNKS)),
             dma((NM,)), dma((NM,)),
             dma((NM,)), dma((NM,)),
-            dma((5,)),
+            dma((NM,)), dma((NM,)),
+            dma((7,)),
         ],
         compiler_params=pltpu.CompilerParams(
             collective_id=0, has_side_effects=True, vmem_limit_bytes=58 * 2**20
@@ -445,14 +460,50 @@
     )(tokens, weight, at, b, ids, panel_of, flags, upstream)
 
 
+def copies(*refs):
+    n = (len(refs) - 2) // 3
+    ins, outs, bufs, (in_sems, out_sems) = refs[:n], refs[n : 2 * n], refs[2 * n : 3 * n], refs[3 * n :]
+    parts = []
+    for i in range(n):
+        cuts = 4 if ins[i].shape[0] * ins[i].shape[1] > 2**18 else 1
+        step = ins[i].shape[0] // cuts
+        for j in range(cuts):
+            r = pl.ds(step * j, step)
+            k = len(parts)
+            parts.append((
+                pltpu.make_async_copy(ins[i].at[r], bufs[i].at[r], in_sems.at[k]),
+                pltpu.make_async_copy(bufs[i].at[r], outs[i].at[r], out_sems.at[k]),
+            ))
+    for c, _ in parts:
+        c.start()
+    for c, d in parts:
+        c.wait()
+        d.start()
+    for _, d in parts:
+        d.wait()
+
+
+def settle(arrays):
+    hbm = pl.BlockSpec(memory_space=pl.ANY)
+    dma = pltpu.SemaphoreType.DMA
+    return pl.pallas_call(
+        copies,
+        out_shape=tuple(jax.ShapeDtypeStruct(a.shape, a.dtype) for a in arrays),
+        in_specs=[hbm] * len(arrays),
+        out_specs=(hbm,) * len(arrays),
+        scratch_shapes=[pltpu.VMEM(a.shape, a.dtype) for a in arrays]
+        + [dma((4 * len(arrays),)), dma((4 * len(arrays),))],
+    )(*arrays)
+
+
 def shards(tokens, base_weight, adapter_a, adapter_b, row_ids, panel_of, stop_flags, upstream):
     per_owner, feats, rank = adapter_a.shape
     vals = upstream.shape[1]
     at = jnp.transpose(adapter_a, (0, 2, 1)).reshape(per_owner * rank, feats)
     b = adapter_b.reshape(per_owner * rank, vals)
-    projected, gradient, down, up = fused(
+    projected, gradient, down, up = settle(fused(
         tokens, base_weight, at, b, row_ids.reshape(1, -1), panel_of.reshape(1, -1), stop_flags, upstream
-    )
+    ))
     return (
         projected,
         gradient,

time: 138 us -> 134 us (0.971)
  local copies, waits for them, and re-layouts: 5.2 us -> 0 us
    unnamed x8 -> x0, local copies, waits for them, and re-layouts: 5.2 us -> none
    pallas_call x0 -> x1, Pallas kernels: none -> 2.35 us  [settle(): pl.pallas_call(copies, out_shape=tuple((jax.ShapeDtypeStruct(a.shape, a.d...]
where the time goes in v3:
time: 134 us
  Pallas kernels  133 us (99%)
    pallas_call x1, Pallas kernels, fused(): pl.pallas_call(kernel, out_shape=(jax.ShapeDtypeStruct((rows, 128), BF16)...  131 us

profile of v3, /device:TPU:1, one launch (start us, length us, event | category | flops | bytes accessed | tf_op | source)
XLA Modules:
  0.0 133.9 jit_solution(5180313666543197011)
XLA Ops:
  0.6 130.9 %shard_map.111 = (bf16[512,128]{1,0:T(8,128)(2,1)}, bf16[512,1024]{1,0:T(8,128)(2,1)}, bf16[128,1024]{1,0:T(8,128)(2,1)}, bf16[128,128]{1,0:T(8,128)(2,1)}) custom-call(bf16[512,1024]{1,0:T(8,128)(2,1)} %tok_hbm.1, bf16[1024,1024]{1,0:T(8,128)(2,1)} %w_hbm.1, bf16[128,1024]{1,0:T(8,128)(2,1)} %bitcast.10, bf16[128,128]{1,0:T(8,128)(2,1)} %bitcast.12, ...), custom_call_target="tpu_custom_call" | custom-call | flops 5000000000 | bytes 10000000 | tf_op jit(solution)/shard_map/pallas_call | solution.py:414
  131.5 2.4 %shard_map.112 = (bf16[512,128]{1,0:T(8,128)(2,1)}, bf16[512,1024]{1,0:T(8,128)(2,1)}, bf16[128,1024]{1,0:T(8,128)(2,1)}, bf16[128,128]{1,0:T(8,128)(2,1)}) custom-call(bf16[512,128]{1,0:T(8,128)(2,1)} %get-tuple-element.12.refs_0_, bf16[512,1024]{1,0:T(8,128)(2,1)} %get-tuple-element.13.refs_1_, bf16[128,1024]{1,0:T(8,128)(2,1)} %get-tuple-element.14.refs_2_, ...), custom_call_target="tpu_custom_call" | custom-call | tf_op jit(solution)/shard_map/pallas_call | solution.py:489

commit v4 on v3

--- a/solution.py
+++ b/solution.py
@@ -15,8 +15,10 @@
 FAR = NZ // 2
 DP = ("y", "z")
 MP = ("x", "core")
-BATCHES = ((0, 9), (9, 13), (13, 15))
+BATCHES = ((0, 9), (9, 13))
 CHUNKS = 2 * FAR - 1
+SUM_HOPS = FAR - 2
+SUMS = 2 * SUM_HOPS
 
 
 def dot(a, b, ca, cb):
@@ -33,8 +35,8 @@
 
 def kernel(tok_hbm, w_hbm, at_ref, b_ref, ids_ref, panel_ref, flags_ref, up_ref,
            proj_ref, tig_ref, down_ref, upg_ref,
-           tok, w, ua, fs, fr, fg, back_place, send, ret, panels, rbuf, rets, pk, rsr, pkf, whole, proj, part, psend, prec,
-           ag_s, ag_r, y_s, y_r, rt_s, rt_r, xs_s, xs_r, xg_s, xg_r, rs_s, rs_r, u_s, u_r, f_s, f_r, b_s, b_r, loc):
+           tok, w, ua, fs, fr, fg, back_place, send, ret, panels, rbuf, rets, pk, rsr, pkf, short, whole, far_rows, far_ranks, proj, part, psend, prec,
+           ag_s, ag_r, y_s, y_r, rt_s, rt_r, xs_s, xs_r, xg_s, xg_r, rs_s, rs_r, u_s, u_r, f_s, f_r, b_s, b_r, fr_s, fr_r, fk_s, fk_r, loc):
     scope = jax.named_scope
     rows, feats = tok.shape
     wide = feats + 128
@@ -43,6 +45,8 @@
     m = xi * NC + ci
     up = {"z": lax.rem(zi + 1, NZ)}
     down = {"z": lax.rem(zi + NZ - 1, NZ)}
+    up2 = {"z": lax.rem(zi + 2, NZ)}
+    down2 = {"z": lax.rem(zi + NZ - 2, NZ)}
 
     def y_peer(d):
         return {"y": lax.rem(yi + d, NY)}
@@ -60,7 +64,7 @@
     w_in.start()
     with scope("entry"):
         bar = pltpu.get_barrier_semaphore()
-        peers = [up, down] + [y_peer(d) for d in range(1, NY)] + [m_peer(d) for d in range(1, NM)]
+        peers = [up, down, up2, down2] + [y_peer(d) for d in range(1, NY)] + [m_peer(d) for d in range(1, NM)]
         for p in peers:
             pl.semaphore_signal(bar, inc=1, device_id=p, device_id_type=pl.DeviceIdType.MESH)
         panels[0, :, :feats] = at_ref[...]
@@ -182,9 +186,13 @@
 
     lane = iota((NY * PAD, 128), 1) < 64
 
+    def masks_of(v):
+        n = v.shape[0] // PAD
+        v = v.astype(F32).reshape(n, PAD, 128)[:, PAD - 1 :, :]
+        return jnp.broadcast_to(v, (n, PAD, 128)).reshape(n * PAD, 128)
+
     def masks(k):
-        v = rbuf[k, :, feats:].astype(F32).reshape(NY, PAD, 128)[:, PAD - 1 :, :]
-        return jnp.broadcast_to(v, (NY, PAD, 128)).reshape(NY * PAD, 128)
+        return masks_of(rbuf[k, :, feats:])
 
     def rows_wait():
         with scope("rows_wait"):
@@ -229,11 +237,13 @@
             ref = pkf.at[k0:k1, pl.ds(pl.multiple_of(src * 8, 8), 8), :]
             remote(ref, ref, xg_s.at[b, d], xg_r.at[b, d], m_peer(d)).wait_recv()
 
+    def spread_of(v, mask):
+        left = iota(v.shape, 1) < 64
+        r = pltpu.roll(v, 64, 1)
+        return (jnp.where(left, v, r) * mask).astype(BF16), (jnp.where(left, r, v) * mask).astype(BF16)
+
     def spread(k):
-        mask = masks(k)
-        v = pkf[k]
-        r = pltpu.roll(v, 64, 1)
-        return (jnp.where(lane, v, r) * mask).astype(BF16), (jnp.where(lane, r, v) * mask).astype(BF16)
+        return spread_of(pkf[k], masks(k))
 
     def sums(k):
         inner, back = spread(k)
@@ -247,6 +257,49 @@
         for q in range(NY):
             rets[q, k, :, :feats] = grad[q * PAD : (q + 1) * PAD]
             rets[q, k, :, feats:] = delta[q * PAD : (q + 1) * PAD]
+
+    def whole_send(i, j0, j1):
+        for j in range(j0, j1):
+            short[j] = pk[13 + j].astype(BF16)
+            whole[m, j] = short[j]
+        for d in range(1, NM):
+            go(short.at[j0:j1], whole.at[m, j0:j1], b_s.at[i, d], b_r.at[i, d], m_peer(d))
+
+    def whole_finish(i, j0, j1):
+        for d in range(1, NM):
+            ref = whole.at[lax.rem(m + NM - d, NM), j0:j1]
+            remote(ref, ref, b_s.at[i, d], b_r.at[i, d], m_peer(d)).wait_recv()
+        for j in range(j0, j1):
+            total = sum(whole[p, j].astype(F32) for p in range(NM))
+            pkf[13 + j] = total.astype(BF16).astype(F32)
+
+    near = NY * PAD
+    far = near // 2
+    far_pieces = (
+        (0, up, 14, pl.ds(0, near), pl.ds(0, near)),
+        (0, down, 13, pl.ds(0, near), pl.ds(0, near)),
+        (1, up2, 15, pl.ds(0, far), pl.ds(near, far)),
+        (1, down2, 15, pl.ds(far, far), pl.ds(near, far)),
+    )
+
+    def far_rows_send():
+        for i, (_, dev, k, src, dst) in enumerate(far_pieces):
+            go(rbuf.at[k, src], far_rows.at[i % 2, dst], fr_s.at[i], fr_r.at[i], dev)
+
+    def far_ranks_send(stage):
+        for i, (at_stage, dev, k, src, dst) in enumerate(far_pieces):
+            if at_stage == stage:
+                go(pkf.at[k, src], far_ranks.at[i % 2, dst], fk_s.at[i], fk_r.at[i], dev)
+
+    def far_sums():
+        for i, (_, dev, k, src, dst) in enumerate(far_pieces):
+            rows_ref, ranks_ref = far_rows.at[i % 2, dst], far_ranks.at[i % 2, dst]
+            remote(rows_ref, rows_ref, fr_s.at[i], fr_r.at[i], dev).wait_recv()
+            remote(ranks_ref, ranks_ref, fk_s.at[i], fk_r.at[i], dev).wait_recv()
+        for v, k in enumerate((12, 11)):
+            inner, back = spread_of(far_ranks[v], masks_of(far_rows[v, :, feats:]))
+            part[k, :, :feats] += dot(back, far_rows[v, :, :feats], 0, 0)
+            part[k, :, feats:] += dot(inner, far_rows[v, :, feats:], 0, 0)
 
     locals_ = [own]
 
@@ -296,30 +349,34 @@
     with scope("ranks_5"):
         first(13)
         first(14)
-        x_send(2)
+        whole_send(0, 0, 2)
     with scope("reduce_1"):
         x_reduce(1)
     ag_step(14)
+    with scope("far_rows_out"):
+        far_rows_send()
     with scope("ranks_6"):
         first(15)
-        for d in range(1, NM):
-            go(pk.at[15], whole.at[m], b_s.at[d], b_r.at[d], m_peer(d))
-        whole[m] = pk[15]
-    with scope("reduce_2"):
-        x_reduce(2)
+        whole_send(1, 2, 3)
+    with scope("whole_0"):
+        whole_finish(0, 0, 2)
+        far_ranks_send(0)
+    with scope("finish_1"):
+        x_finish(1)
+        sums(12)
+        sums(11)
+    with scope("whole_1"):
+        whole_finish(1, 2, 3)
+        far_ranks_send(1)
     with scope("rows_back_a"):
-        for k in range(1, 5):
+        for k in range(1, 4):
             rows_back(k)
-    with scope("finish_last"):
-        for d in range(1, NM):
-            ref = whole.at[lax.rem(m + NM - d, NM)]
-            remote(ref, ref, b_s.at[d], b_r.at[d], m_peer(d)).wait_recv()
-        pkf[15] = sum(whole[j] for j in range(NM)).astype(BF16).astype(F32)
-
-    def piece(w, c):
-        s, h = FAR - (c + 1) // 2, (c % 2 if c else 0)
-        hh = h if w == 0 else 1 - h
-        return (above(s) if w == 0 else below(s)), pl.ds(half * hh, half)
+    with scope("far_sums"):
+        far_sums()
+
+    def piece(v, c):
+        s, h = SUM_HOPS - c // 2, c % 2
+        return (above(s) if v == 0 else below(s)), pl.ds(half * (h if v == 0 else 1 - h), half)
 
     def rs_step(c):
         with scope(f"sum_hop_{c}"):
@@ -333,32 +390,25 @@
                 psend[v, c] = x.astype(BF16)
                 go(psend.at[v, c], prec.at[v, c], rs_s.at[v, c], rs_r.at[v, c], dev)
 
-    sums(15)
     rs_step(0)
-    with scope("finish_2"):
-        x_finish(2)
-    sums(14)
-    sums(13)
     rs_step(1)
-    with scope("finish_1"):
-        x_finish(1)
-    with scope("rows_back_b"):
-        for k in range(5, 8):
-            rows_back(k)
-        ret_send(0, 0, 8)
-    rs_step(2)
-    for i, s in enumerate(range(6, 0, -1)):
+    for i, s in enumerate(range(SUM_HOPS - 1, 0, -1)):
         with scope("sums"):
             sums(2 * s)
             sums(2 * s - 1)
-        rs_step(3 + 2 * i)
-        if i < 4:
+        rs_step(2 + 2 * i)
+        if i == 0:
+            with scope("rows_back_b"):
+                for k in range(4, 8):
+                    rows_back(k)
+                ret_send(0, 0, 8)
+        if i in (1, 2):
             with scope("rows_back_c"):
-                rows_back(8 + 2 * i)
-                rows_back(9 + 2 * i)
+                for k in range(4):
+                    rows_back(4 + 4 * i + k)
+                if i == 2:
+                    ret_send(1, 8, 16)
         if i == 3:
-            ret_send(1, 8, 16)
-        if i == 4:
             with scope("base_wait"):
                 acc = fs[m]
                 for d in range(1, NM):
@@ -366,7 +416,7 @@
                     remote(fr.at[src], fr.at[src], f_s.at[d], f_r.at[d], m_peer(d)).wait_recv()
                     acc = acc + fr[src]
                 fs[m] = acc
-        rs_step(4 + 2 * i)
+        rs_step(3 + 2 * i)
     sums(0)
     with scope("returned_wait"):
         ret_wait(0, 0, 8)
@@ -384,12 +434,12 @@
         proj_out.start()
     with scope("last_sums"):
         for v, dev in enumerate((up, down)):
-            for c in (CHUNKS - 2, CHUNKS - 1):
+            for c in (SUMS - 2, SUMS - 1):
                 ref = prec.at[v, c]
                 remote(ref, ref, rs_s.at[v, c], rs_r.at[v, c], dev).wait_recv()
         for p in range(2):
             scale = SCALE * (1 - flags_ref[p]).astype(F32)
-            c0, c1 = (CHUNKS - 1, CHUNKS - 2) if p == 0 else (CHUNKS - 2, CHUNKS - 1)
+            c0, c1 = (SUMS - 2, SUMS - 1) if p == 0 else (SUMS - 1, SUMS - 2)
             r = slice(p * half, (p + 1) * half)
             v = scale * (part[0, r] + prec[0, c0].astype(F32) + prec[1, c1].astype(F32))
             down_ref[r] = v[:, :feats].astype(BF16)
@@ -437,20 +487,25 @@
             pltpu.VMEM((NZ, group, 128), F32),
             pltpu.VMEM((NM, NZ, group // NM, 128), F32),
             pltpu.VMEM((NZ, group, 128), F32),
-            pltpu.VMEM((NM, group, 128), F32),
+            pltpu.VMEM((3, group, 128), BF16),
+            pltpu.VMEM((NM, 3, group, 128), BF16),
+            pltpu.VMEM((2, group + group // 2, wide), BF16),
+            pltpu.VMEM((2, group + group // 2, 128), F32),
             pltpu.VMEM((rows, 128), BF16),
             pltpu.VMEM((NZ, n, wide), F32),
-            pltpu.VMEM((2, CHUNKS, half, wide), BF16),
-            pltpu.VMEM((2, CHUNKS, half, wide), BF16),
+            pltpu.VMEM((2, SUMS, half, wide), BF16),
+            pltpu.VMEM((2, SUMS, half, wide), BF16),
             dma((2, CHUNKS)), dma((2, CHUNKS)),
             dma((NY,)), dma((NY,)),
             dma((2, NY)), dma((2, NY)),
             dma((nb, NM)), dma((nb, NM)),
             dma((nb, NM)), dma((nb, NM)),
-            dma((2, CHUNKS)), dma((2, CHUNKS)),
+            dma((2, SUMS)), dma((2, SUMS)),
             dma((NM,)), dma((NM,)),
             dma((NM,)), dma((NM,)),
-            dma((NM,)), dma((NM,)),
+            dma((2, NM)), dma((2, NM)),
+            dma((4,)), dma((4,)),
+            dma((4,)), dma((4,)),
             dma((7,)),
         ],
         compiler_params=pltpu.CompilerParams(

time: 134 us -> 127 us (0.948)
  Pallas kernels: 133 us -> 126 us
    pallas_call x1, Pallas kernels: 131 us -> 123 us  [fused(): pl.pallas_call(kernel, out_shape=(jax.ShapeDtypeStruct((rows, 128), BF16)...]
where the time goes in v4:
time: 127 us; the launch traced here: 126 us
  Pallas kernels  126 us (99%)
    pallas_call x1, Pallas kernels, fused(): pl.pallas_call(kernel, out_shape=(jax.ShapeDtypeStruct((rows, 128), BF16)...  123 us

profile of v4, /device:TPU:1, one launch (start us, length us, event | category | flops | bytes accessed | tf_op | source)
XLA Modules:
  0.0 126.2 jit_solution(7414174239577901192)
XLA Ops:
  0.6 123.2 %shard_map.111 = (bf16[512,128]{1,0:T(8,128)(2,1)}, bf16[512,1024]{1,0:T(8,128)(2,1)}, bf16[128,1024]{1,0:T(8,128)(2,1)}, bf16[128,128]{1,0:T(8,128)(2,1)}) custom-call(bf16[512,1024]{1,0:T(8,128)(2,1)} %tok_hbm.1, bf16[1024,1024]{1,0:T(8,128)(2,1)} %w_hbm.1, bf16[128,1024]{1,0:T(8,128)(2,1)} %bitcast.10, bf16[128,128]{1,0:T(8,128)(2,1)} %bitcast.12, ...), custom_call_target="tpu_custom_call" | custom-call | flops 5000000000 | bytes 10000000 | tf_op jit(solution)/shard_map/pallas_call | solution.py:464
  123.8 2.4 %shard_map.112 = (bf16[512,128]{1,0:T(8,128)(2,1)}, bf16[512,1024]{1,0:T(8,128)(2,1)}, bf16[128,1024]{1,0:T(8,128)(2,1)}, bf16[128,128]{1,0:T(8,128)(2,1)}) custom-call(bf16[512,128]{1,0:T(8,128)(2,1)} %get-tuple-element.12.refs_0_, bf16[512,1024]{1,0:T(8,128)(2,1)} %get-tuple-element.13.refs_1_, bf16[128,1024]{1,0:T(8,128)(2,1)} %get-tuple-element.14.refs_2_, ...), custom_call_target="tpu_custom_call" | custom-call | tf_op jit(solution)/shard_map/pallas_call | solution.py:544

commit v5 on v4

--- a/solution.py
+++ b/solution.py
@@ -33,14 +33,14 @@
     return 0 if s == 0 else (NZ - 1 if s == FAR else 2 * s)
 
 
-def kernel(tok_hbm, w_hbm, at_ref, b_ref, ids_ref, panel_ref, flags_ref, up_ref,
+def kernel(tok_hbm, w_hbm, at_hbm, b_hbm, ids_hbm, panel_hbm, flags_ref, up_hbm,
            proj_ref, tig_ref, down_ref, upg_ref,
-           tok, w, ua, fs, fr, fg, back_place, send, ret, panels, rbuf, rets, pk, rsr, pkf, short, whole, far_rows, far_ranks, proj, part, psend, prec,
+           tok, w, ids_ref, panel_ref, up_ref, ua, fs, fr, fg, back_place, send, ret, panels, rbuf, rets, pk, rsr, pkf, short, whole, far_rows, far_ranks, proj, part, psend, prec,
            ag_s, ag_r, y_s, y_r, rt_s, rt_r, xs_s, xs_r, xg_s, xg_r, rs_s, rs_r, u_s, u_r, f_s, f_r, b_s, b_r, fr_s, fr_r, fk_s, fk_r, loc):
     scope = jax.named_scope
     rows, feats = tok.shape
     wide = feats + 128
-    half = at_ref.shape[0] // 2
+    half = at_hbm.shape[0] // 2
     yi, zi, xi, ci = (lax.axis_index(n) for n in ("y", "z", "x", "core"))
     m = xi * NC + ci
     up = {"z": lax.rem(zi + 1, NZ)}
@@ -58,17 +58,25 @@
     def lanes(p):
         return pl.ds(pl.multiple_of(p * 128, 128), 128)
 
-    tok_in = pltpu.make_async_copy(tok_hbm, tok, loc.at[3])
-    tok_in.start()
-    w_in = pltpu.make_async_copy(w_hbm, w, loc.at[4])
-    w_in.start()
+    def load(src, dst, i):
+        c = pltpu.make_async_copy(src, dst, loc.at[i])
+        c.start()
+        return c
+
     with scope("entry"):
         bar = pltpu.get_barrier_semaphore()
         peers = [up, down, up2, down2] + [y_peer(d) for d in range(1, NY)] + [m_peer(d) for d in range(1, NM)]
         for p in peers:
             pl.semaphore_signal(bar, inc=1, device_id=p, device_id_type=pl.DeviceIdType.MESH)
-        panels[0, :, :feats] = at_ref[...]
-        panels[0, :, feats:] = b_ref[...]
+        panels_in = [
+            load(at_hbm, panels.at[0, :, pl.ds(0, feats)], 7),
+            load(b_hbm, panels.at[0, :, pl.ds(feats, 128)], 8),
+        ]
+        routes_in = [load(ids_hbm, ids_ref, 9), load(panel_hbm, panel_ref, 10), load(up_hbm, up_ref, 11)]
+        tok_in = load(tok_hbm, tok, 3)
+        w_in = load(w_hbm, w, 4)
+        for c in panels_in:
+            c.wait()
         pl.semaphore_wait(bar, len(peers))
 
     started = []
@@ -111,6 +119,8 @@
         return jnp.where(cond, 1.0, 0.0)
 
     with scope("routing"):
+        for c in routes_in:
+            c.wait()
         n_panels = panel_ref.shape[1]
         owners = NY * NZ
         rank = 64
@@ -134,55 +144,72 @@
         pick = hot((iota((owners, 128), 1) // rank).astype(F32) == which)
         last = iota((NZ * PAD, 128), 0) % PAD == PAD - 1
         tok_in.wait()
+    def rows_out(q):
+        place = hot(iota((NZ * PAD, rows), 0) + q * NZ * PAD == slot).astype(BF16)
+        t = dot(place, tok[...], 1, 0).astype(BF16)
+        u = dot(place, up_ref[...], 1, 0)
+        marks = jnp.broadcast_to(pick[q * NZ : (q + 1) * NZ].reshape(NZ, 1, 128), (NZ, PAD, 128))
+        u = jnp.where(last, marks.reshape(NZ * PAD, 128), u).astype(BF16)
+        send[q, :, :, :feats] = t.reshape(NZ, PAD, feats)
+        send[q, :, :, feats:] = u.reshape(NZ, PAD, 128)
+
+    with scope("rows_placed"):
+        rows_out(0)
+        rows_out(1)
+    ag_step(0)
     with scope("rows_out"):
-        for q in range(NY):
-            place = hot(iota((NZ * PAD, rows), 0) + q * NZ * PAD == slot).astype(BF16)
-            t = dot(place, tok[...], 1, 0).astype(BF16)
-            u = dot(place, up_ref[...], 1, 0)
-            marks = jnp.broadcast_to(pick[q * NZ : (q + 1) * NZ].reshape(NZ, 1, 128), (NZ, PAD, 128))
-            u = jnp.where(last, marks.reshape(NZ * PAD, 128), u).astype(BF16)
-            send[q, :, :, :feats] = t.reshape(NZ, PAD, feats)
-            send[q, :, :, feats:] = u.reshape(NZ, PAD, 128)
+        rows_out(2)
+        rows_out(3)
         mine_rows = pl.ds(pl.multiple_of(yi * PAD, PAD), PAD)
         for d in range(1, NY):
             go(send.at[lax.rem(yi + d, NY)], rbuf.at[:, mine_rows, :], y_s.at[d], y_r.at[d], y_peer(d))
         own = pltpu.make_async_copy(send.at[yi], rbuf.at[:, mine_rows, :], loc.at[0])
         own.start()
-    ag_step(0)
     with scope("cotangents_out"):
         for d in range(1, NM):
             go(up_ref, ua.at[:, lanes(m)], u_s.at[d], u_r.at[d], m_peer(d))
         ua[:, lanes(m)] = up_ref[...]
+    ag_step(1)
+
+    def base(j):
+        r = dot(tok[...], w[:, 256 * j : 256 * j + 256], 1, 0)
+        fs[2 * j] = r[:, :128]
+        fs[2 * j + 1] = r[:, 128:]
+
+    with scope("base"):
         w_in.wait()
-    with scope("base"):
-        for j in range(NM // 2):
-            r = dot(tok[...], w[:, 256 * j : 256 * j + 256], 1, 0)
-            fs[2 * j] = r[:, :128]
-            fs[2 * j + 1] = r[:, 128:]
-    ag_step(1)
-    with scope("base_out"):
-        for d in range(1, NM):
-            p = lax.rem(m + d, NM)
-            go(fs.at[p], fr.at[m], f_s.at[d], f_r.at[d], m_peer(d))
+        base(0)
+        base(1)
     ag_step(2)
+    with scope("base_more"):
+        base(2)
+        base(3)
+    ag_step(3)
     with scope("row_places"):
         ones = jnp.ones((owners, 128), BF16)
         blocks = dot((block_hot * iota((owners, rows), 0).astype(F32)).astype(BF16), ones, 0, 0)
         slot_col = blocks * PAD + dot(counts.astype(BF16), ones, 0, 0)
-        for j in range(owners * PAD // 128):
-            back_place[:, 128 * j : 128 * j + 128] = hot(
-                (iota((rows, 128), 1) + 128 * j).astype(F32) == slot_col
-            ).astype(BF16)
-    ag_step(3)
+
+    def row_places(j):
+        back_place[:, 128 * j : 128 * j + 128] = hot(
+            (iota((rows, 128), 1) + 128 * j).astype(F32) == slot_col
+        ).astype(BF16)
+
+    for j in range(4):
+        row_places(j)
+    ag_step(4)
+    for j in range(4, 8):
+        row_places(j)
     with scope("cotangents_wait"):
         for d in range(1, NM):
             ref = ua.at[:, lanes(lax.rem(m + NM - d, NM))]
             remote(ref, ref, u_s.at[d], u_r.at[d], m_peer(d)).wait_recv()
-    ag_step(4)
-    with scope("base_gradient"):
-        for j in range(2):
-            fg[256 * j : 256 * j + 256] = dot(ua[256 * j : 256 * j + 256], w[...], 1, 1)
-    ag_step(5)
+    for c in range(4):
+        ag_step(5 + c)
+        with scope("base_gradient"):
+            r = pl.ds(256 * c, 256)
+            fg[:, r] = dot(ua[...], w[r, :], 1, 1)
+    ag_step(9)
 
     lane = iota((NY * PAD, 128), 1) < 64
 
@@ -316,61 +343,52 @@
             ref = ret.at[lax.rem(yi + NY - d, NY), k0:k1]
             remote(ref, ref, rt_s.at[i, d], rt_r.at[i, d], y_peer(d)).wait_recv()
 
-    for c in range(6, 9):
-        ag_step(c)
     rows_wait()
     with scope("ranks_0"):
-        for k in range(3):
-            first(k)
-    ag_step(9)
-    with scope("ranks_1"):
-        for k in range(3, 6):
+        for k in (9, 10, 7, 8):
             first(k)
     ag_step(10)
+    with scope("ranks_1"):
+        for k in (5, 6, 3):
+            first(k)
+    ag_step(11)
     with scope("ranks_2"):
-        for k in range(6, 9):
-            first(k)
-        x_send(0)
-    ag_step(11)
-    with scope("ranks_3"):
-        first(9)
-        first(10)
-    with scope("reduce_0"):
-        x_reduce(0)
-    ag_step(12)
-    with scope("ranks_4"):
         first(11)
         first(12)
         x_send(1)
-    with scope("finish_0"):
-        x_finish(0)
-    rows_back(0)
+        first(4)
+    ag_step(12)
+    with scope("ranks_3"):
+        for k in range(3):
+            first(k)
+        x_send(0)
+        x_reduce(1)
     ag_step(13)
-    with scope("ranks_5"):
+    with scope("ranks_4"):
         first(13)
         first(14)
         whole_send(0, 0, 2)
-    with scope("reduce_1"):
-        x_reduce(1)
+        x_finish(1)
+        sums(12)
+        sums(11)
     ag_step(14)
     with scope("far_rows_out"):
         far_rows_send()
-    with scope("ranks_6"):
+    with scope("ranks_5"):
         first(15)
         whole_send(1, 2, 3)
     with scope("whole_0"):
         whole_finish(0, 0, 2)
         far_ranks_send(0)
-    with scope("finish_1"):
-        x_finish(1)
-        sums(12)
-        sums(11)
+        x_reduce(0)
     with scope("whole_1"):
         whole_finish(1, 2, 3)
         far_ranks_send(1)
-    with scope("rows_back_a"):
-        for k in range(1, 4):
-            rows_back(k)
+    with scope("finish_0"):
+        sums(10)
+        sums(9)
+        x_finish(0)
+        rows_back(0)
     with scope("far_sums"):
         far_sums()
 
@@ -392,23 +410,30 @@
 
     rs_step(0)
     rs_step(1)
+    with scope("base_out"):
+        for d in range(1, NM):
+            p = lax.rem(m + d, NM)
+            go(fs.at[p], fr.at[m], f_s.at[d], f_r.at[d], m_peer(d))
     for i, s in enumerate(range(SUM_HOPS - 1, 0, -1)):
         with scope("sums"):
-            sums(2 * s)
-            sums(2 * s - 1)
+            if i:
+                sums(2 * s)
+                sums(2 * s - 1)
         rs_step(2 + 2 * i)
         if i == 0:
             with scope("rows_back_b"):
-                for k in range(4, 8):
+                for k in range(1, 5):
+                    rows_back(k)
+        if i == 1:
+            with scope("rows_back_c"):
+                for k in range(5, 8):
                     rows_back(k)
                 ret_send(0, 0, 8)
-        if i in (1, 2):
-            with scope("rows_back_c"):
-                for k in range(4):
-                    rows_back(4 + 4 * i + k)
-                if i == 2:
-                    ret_send(1, 8, 16)
-        if i == 3:
+        if i == 2:
+            with scope("rows_back_d"):
+                for k in range(10, 13):
+                    rows_back(k)
+        if i == 4:
             with scope("base_wait"):
                 acc = fs[m]
                 for d in range(1, NM):
@@ -417,6 +442,14 @@
                     acc = acc + fr[src]
                 fs[m] = acc
         rs_step(3 + 2 * i)
+        if i in (0, 1):
+            with scope("rows_back_e"):
+                rows_back(8 + i)
+        if i == 2:
+            with scope("rows_back_f"):
+                for k in range(13, 16):
+                    rows_back(k)
+                ret_send(1, 8, 16)
     sums(0)
     with scope("returned_wait"):
         ret_wait(0, 0, 8)
@@ -469,11 +502,14 @@
             jax.ShapeDtypeStruct((n, feats), BF16),
             jax.ShapeDtypeStruct((n, 128), BF16),
         ),
-        in_specs=[hbm, hbm, vm, vm, vm, vm, pl.BlockSpec(memory_space=pltpu.SMEM), vm],
+        in_specs=[hbm, hbm, hbm, hbm, hbm, hbm, pl.BlockSpec(memory_space=pltpu.SMEM), hbm],
         out_specs=(hbm, hbm, vm, vm),
         scratch_shapes=[
             pltpu.VMEM((rows, feats), BF16),
             pltpu.VMEM(weight.shape, BF16),
+            pltpu.VMEM(ids.shape, jnp.int32),
+            pltpu.VMEM(panel_of.shape, jnp.int32),
+            pltpu.VMEM(upstream.shape, BF16),
             pltpu.VMEM((rows, NM * 128), BF16),
             pltpu.VMEM((NM, rows, 128), F32),
             pltpu.VMEM((NM, rows, 128), F32),
@@ -506,7 +542,7 @@
             dma((2, NM)), dma((2, NM)),
             dma((4,)), dma((4,)),
             dma((4,)), dma((4,)),
-            dma((7,)),
+            dma((12,)),
         ],
         compiler_params=pltpu.CompilerParams(
             collective_id=0, has_side_effects=True, vmem_limit_bytes=58 * 2**20

time: 127 us -> 125 us (0.984)
  Pallas kernels: 126 us -> 122 us
    pallas_call x1, Pallas kernels: 123 us -> 120 us  [fused(): pl.pallas_call(kernel, out_shape=(jax.ShapeDtypeStruct((rows, 128), BF16)...]
where the time goes in v5:
time: 125 us; the launch traced here: 123 us
  Pallas kernels  122 us (98%)
    pallas_call x1, Pallas kernels, fused(): pl.pallas_call(kernel, out_shape=(jax.ShapeDtypeStruct((rows, 128), BF16)...  120 us

profile of v5, /device:TPU:1, one launch (start us, length us, event | category | flops | bytes accessed | tf_op | source)
XLA Modules:
  0.0 122.9 jit_solution(9028685844483279948)
XLA Ops:
  0.6 119.9 %shard_map.111 = (bf16[512,128]{1,0:T(8,128)(2,1)}, bf16[512,1024]{1,0:T(8,128)(2,1)}, bf16[128,1024]{1,0:T(8,128)(2,1)}, bf16[128,128]{1,0:T(8,128)(2,1)}) custom-call(bf16[512,1024]{1,0:T(8,128)(2,1)} %tok_hbm.1, bf16[1024,1024]{1,0:T(8,128)(2,1)} %w_hbm.1, bf16[128,1024]{1,0:T(8,128)(2,1)} %bitcast.10, bf16[128,128]{1,0:T(8,128)(2,1)} %bitcast.12, ...), custom_call_target="tpu_custom_call" | custom-call | flops 5000000000 | bytes 10000000 | tf_op jit(solution)/shard_map/pallas_call | solution.py:497
  120.6 2.4 %shard_map.112 = (bf16[512,128]{1,0:T(8,128)(2,1)}, bf16[512,1024]{1,0:T(8,128)(2,1)}, bf16[128,1024]{1,0:T(8,128)(2,1)}, bf16[128,128]{1,0:T(8,128)(2,1)}) custom-call(bf16[512,128]{1,0:T(8,128)(2,1)} %get-tuple-element.12.refs_0_, bf16[512,1024]{1,0:T(8,128)(2,1)} %get-tuple-element.13.refs_1_, bf16[128,1024]{1,0:T(8,128)(2,1)} %get-tuple-element.14.refs_2_, ...), custom_call_target="tpu_custom_call" | custom-call | tf_op jit(solution)/shard_map/pallas_call | solution.py:580

commit v6 on v5

--- a/solution.py
+++ b/solution.py
@@ -380,15 +380,13 @@
     with scope("whole_0"):
         whole_finish(0, 0, 2)
         far_ranks_send(0)
-        x_reduce(0)
     with scope("whole_1"):
         whole_finish(1, 2, 3)
         far_ranks_send(1)
-    with scope("finish_0"):
+    with scope("reduce_0"):
+        x_reduce(0)
         sums(10)
         sums(9)
-        x_finish(0)
-        rows_back(0)
     with scope("far_sums"):
         far_sums()
 
@@ -422,7 +420,8 @@
         rs_step(2 + 2 * i)
         if i == 0:
             with scope("rows_back_b"):
-                for k in range(1, 5):
+                x_finish(0)
+                for k in range(5):
                     rows_back(k)
         if i == 1:
             with scope("rows_back_c"):

time: 125 us -> 125 us (level)
  no operation moved by 1% of the time
where the time goes in v6:
time: 125 us; the launch traced here: 123 us
  Pallas kernels  122 us (98%)
    pallas_call x1, Pallas kernels, fused(): pl.pallas_call(kernel, out_shape=(jax.ShapeDtypeStruct((rows, 128), BF16)...  120 us

profile of v6, /device:TPU:1, one launch (start us, length us, event | category | flops | bytes accessed | tf_op | source)
XLA Modules:
  0.0 123.0 jit_solution(14645959615934694403)
XLA Ops:
  0.6 120.0 %shard_map.111 = (bf16[512,128]{1,0:T(8,128)(2,1)}, bf16[512,1024]{1,0:T(8,128)(2,1)}, bf16[128,1024]{1,0:T(8,128)(2,1)}, bf16[128,128]{1,0:T(8,128)(2,1)}) custom-call(bf16[512,1024]{1,0:T(8,128)(2,1)} %tok_hbm.1, bf16[1024,1024]{1,0:T(8,128)(2,1)} %w_hbm.1, bf16[128,1024]{1,0:T(8,128)(2,1)} %bitcast.10, bf16[128,128]{1,0:T(8,128)(2,1)} %bitcast.12, ...), custom_call_target="tpu_custom_call" | custom-call | flops 5000000000 | bytes 10000000 | tf_op jit(solution)/shard_map/pallas_call | solution.py:496
  120.7 2.4 %shard_map.112 = (bf16[512,128]{1,0:T(8,128)(2,1)}, bf16[512,1024]{1,0:T(8,128)(2,1)}, bf16[128,1024]{1,0:T(8,128)(2,1)}, bf16[128,128]{1,0:T(8,128)(2,1)}) custom-call(bf16[512,128]{1,0:T(8,128)(2,1)} %get-tuple-element.12.refs_0_, bf16[512,1024]{1,0:T(8,128)(2,1)} %get-tuple-element.13.refs_1_, bf16[128,1024]{1,0:T(8,128)(2,1)} %get-tuple-element.14.refs_2_, ...), custom_call_target="tpu_custom_call" | custom-call | tf_op jit(solution)/shard_map/pallas_call | solution.py:579
